TPU v7x, 512 devices: a whole 4x4x16 slice. The times are simulated.
512 devices in a mesh: tm: 32 (over z, core), tp: 16 (over y, x).
Axes of the slice: x: 4, y: 4, z: 16, core: 2. Of those that a mesh axis runs over, the one named last changes fastest.
Arguments:
- latents: float32 [32, 256, 64], P('tm', 'tp'), may hold values from -6 to 6
- start_latent: float32 [256, 64], P('tp'), may hold values from -6 to 6
- t_index: int32 [32], P('tm'), may hold values from 0 to 999
- dt_units: int32 [32], P('tm'), may hold values from 6 to 25
- w_time: bfloat16 [256, 9216], P(None, 'tp'), may hold values from -0.375 to 0.375
- w_in: bfloat16 [64, 3072], replicated, may hold values from -0.75 to 0.75
- w_up: bfloat16 [3072, 6144], P(None, 'tp'), may hold values from -0.109375 to 0.109375
- w_down: bfloat16 [6144, 3072], P('tp'), may hold values from -0.078125 to 0.078125
- w_out: bfloat16 [3072, 64], replicated, may hold values from -0.109375 to 0.109375
Outputs:
- new_latents: float32 [32, 256, 64], P('tm', 'tp')
- step_error: float32 [32], P('tm')
All inputs are finite; a program needn't handle non-finite values.
Results may differ from a plain program's by a relative error of at most 0.0025.
Values may be sent and summed in bfloat16 or wider, within the bound.
No kernel may reach another device: no remote copies, remote signals or barrier semaphores. Data moves between devices by JAX's collectives and lax.ppermute only.
A program may use at most 64 MiB of HBM per device.

v0:
```python
import jax
import jax.numpy as jnp
from jax import lax
from jax.sharding import PartitionSpec as P


def prefix(value, axis, join, neutral):
    count, mine = (lax.axis_size(axis), lax.axis_index(axis))
    pieces = lax.all_gather(value, axis)
    running = jnp.full_like(value, 0) + jnp.asarray(neutral, value.dtype)

    def turn(position, running):
        longer = join(running, pieces[position])
        return jnp.where(position < mine, longer, running)

    return lax.fori_loop(0, count - 1, turn, running)


def layer_norm(hidden, scale, shift):
    center = hidden - jnp.mean(hidden, axis=-1, keepdims=True)
    spread = jnp.mean(center * center, axis=-1, keepdims=True)
    return (center / jnp.sqrt(spread + 1e-06) * (1.0 + scale) + shift).astype(jnp.bfloat16)


def local(latents, start_latent, t_index, dt_units, w_time, w_in, w_up, w_down, w_out):
    width = w_in.shape[1]
    tok_rows = latents.shape[1]
    channels = latents.shape[2]
    half = w_time.shape[0] // 2
    freqs = jnp.exp(-jnp.log(10000.0) * jnp.arange(half).astype(jnp.float32) / half)
    angle = t_index.astype(jnp.float32)[:, None] * freqs[None, :]
    emb = jnp.concatenate([jnp.cos(angle), jnp.sin(angle)], axis=1).astype(jnp.bfloat16)
    mod_part = jnp.dot(emb, w_time, preferred_element_type=jnp.float32)
    mods = lax.all_gather(mod_part, "tp", axis=1, tiled=True)
    shift = mods[:, :width]
    scale = mods[:, width : 2 * width]
    gate = mods[:, 2 * width :]
    own_rows = latents[0].astype(jnp.bfloat16)
    hidden = jnp.dot(own_rows, w_in, preferred_element_type=jnp.float32)
    normed = layer_norm(hidden, scale, shift)
    act = jax.nn.gelu(
        jnp.dot(
            lax.all_gather(normed, "tp", axis=0, tiled=True),
            w_up,
            preferred_element_type=jnp.float32,
        ),
        approximate=True,
    ).astype(jnp.bfloat16)
    out_full = w_out.astype(jnp.float32)
    branch = lax.psum_scatter(
        jnp.dot(act, w_down, preferred_element_type=jnp.float32),
        "tp",
        scatter_dimension=0,
        tiled=True,
    )
    mixed = hidden + gate * branch
    drift = jnp.dot(mixed, out_full, precision=lax.Precision.HIGHEST)
    weighted = (dt_units.astype(jnp.float32) * 0.0078125)[:, None, None] * drift[None]
    zeros = jnp.zeros_like(weighted)

    def add_terms(earlier, later):
        return earlier + later

    before = prefix(weighted, "tm", add_terms, zeros)
    new_latents = start_latent[None] + before
    change = new_latents - latents
    local_sum = jnp.sum(change * change)
    total = lax.psum(local_sum, "tp")
    count = tok_rows * lax.axis_size("tp") * channels
    step_error = (total / count).reshape(1)
    return (new_latents, step_error)


def solution(mesh):
    in_specs = (
        P("tm", "tp", None),
        P("tp", None),
        P("tm"),
        P("tm"),
        P(None, "tp"),
        P(),
        P(None, "tp"),
        P("tp", None),
        P(),
    )
    out_specs = (P("tm", "tp", None), P("tm"))
    return jax.shard_map(local, mesh=mesh, in_specs=in_specs, out_specs=out_specs, check_vma=False)
```

profile of v0, /device:TPU:2, one launch (start us, length us, event | category | flops | bytes accessed | tf_op | source)
XLA Modules:
  0.0 324.3 jit_solution(14585137377911968047)
XLA Ops:
  7.2 0.0 copy-start
  7.2 0.0 all-gather.4.cloned.1.call-start
  7.2 1.4 fusion.25
  8.7 0.2 multiply_reduce_fusion
  9.7 1.2 convolution_reduce_fusion
  10.8 1.3 dynamic-slice
  12.8 0.3 dynamic-update-slice
  13.1 72.1 %all-reduce = f32[9216]{0:T(1024)S(1)} all-reduce(f32[9216]{0:T(1024)S(1)} %dynamic-update-slice), channel_id=2, replica_groups=mesh['tm'=32,'tp'=16] {'tp'}, use_global_device_ids=true, to_apply=%add | all-reduce | flops 9216 | bytes 73728
  85.1 0.7 add_convert_fusion
  85.9 0.0 all-gather.4.cloned.1.call-update
  85.9 0.0 reduce-scatter.2.cloned.1.call-start
  85.9 60.8 %all-gather.4.cloned.1.call-done = bf16[256,3072]{1,0:T(8,128)(2,1)} async-done(((bf16[16,3072]{1,0:T(8,128)(2,1)}), bf16[256,3072]{1,0:T(8,128)(2,1)}) %all-gather.4.cloned.1.call-update) | async-done | bytes 1572880 | tf_op jit(solution)/shard_map/all_gather | solution.py:43
  146.8 0.0 copy-done
  146.8 5.7 %fusion.8 = f32[256,3072]{1,0:T(8,128)} fusion(bf16[384,3072]{1,0:T(8,128)(2,1)S(1)} %copy-done, bf16[256,3072]{1,0:T(8,128)(2,1)} %all-gather.4.cloned.1.call-done, bf16[3072,384]{1,0:T(8,128)(2,1)} %param.17), kind=kOutput, calls=%fused_computation.12 | convolution fusion | flops 1208844288 | bytes 9437184 | tf_op jit(solution)/shard_map/dot_general | solution.py:51
  152.5 0.0 copy-start.1
  152.5 0.0 copy-start.2
  152.5 0.0 copy-start.3
  152.5 0.0 reduce-scatter.2.cloned.1.call-update
  153.3 90.1 %reduce-scatter.2.cloned.1.call-done = f32[16,3072]{1,0:T(8,128)} async-done(((f32[256,3072]{1,0:T(8,128)}), f32[16,3072]{1,0:T(8,128)}) %reduce-scatter.2.cloned.1.call-update) | async-done | bytes 196624 | tf_op jit(solution)/shard_map/reduce_scatter | solution.py:50
  243.4 0.0 copy-done.1
  243.4 1.3 convolution_multiply_fusion
  244.7 31.7 %all-gather.1 = f32[512,64]{1,0:T(8,128)S(1)} all-gather(f32[16,64]{1,0:T(8,128)S(1)} %convolution_multiply_fusion), channel_id=3, replica_groups=mesh['tm'=32,'tp'=16] {'tm'}, dimensions={0}, use_global_device_ids=true | all-gather | bytes 135168 | tf_op jit(solution)/shard_map/all_gather | solution.py:9
  276.4 1.1 while.14
  277.5 0.0 copy-done.2
  277.5 0.0 copy-done.3
  277.5 1.2 multiply_reduce_fusion.1
  278.7 37.0 %psum.7 = f32[]{:T(128)} all-reduce(f32[]{:T(128)} %get-tuple-element.109), channel_id=1, replica_groups=mesh['tm'=32,'tp'=16] {'tp'}, use_global_device_ids=true, to_apply=%region_6.7 | all-reduce | flops 1 | bytes 8 | tf_op jit(solution)/shard_map/psum | solution.py:68
  (39 shorter events, 0.4 us)
Async XLA Ops:
  7.2 139.6 %copy-start = (bf16[384,3072]{1,0:T(8,128)(2,1)S(1)}, bf16[384,3072]{1,0:T(8,128)(2,1)}, u32[]{:S(2)}) copy-start(bf16[384,3072]{1,0:T(8,128)(2,1)} %param.18) | copy-start | bytes 7077892
  7.2 139.6 %all-gather.4.cloned.1.call-start = ((), (), s32[]{:S(2)}) async-start(), calls=%async_computation.1 | async-start | bytes 1671168 | tf_op jit(solution)/shard_map/all_gather | solution.py:43
  85.9 157.5 %reduce-scatter.2.cloned.1.call-start = ((), (), s32[]{:S(2)}) async-start(), calls=%async_computation.2 | async-start | bytes 3342336 | tf_op jit(solution)/shard_map/reduce_scatter | solution.py:50
  152.5 90.8 %copy-start.1 = (bf16[3072,64]{0,1:T(8,128)(2,1)S(1)}, bf16[3072,64]{0,1:T(8,128)(2,1)}, u32[]{:S(2)}) copy-start(bf16[3072,64]{0,1:T(8,128)(2,1)} %param.19) | copy-start | bytes 1179652
  152.5 125.0 %copy-start.2 = (f32[1,16,64]{2,1,0:T(8,128)S(1)}, f32[1,16,64]{2,1,0:T(8,128)}, u32[]{:S(2)}) copy-start(f32[1,16,64]{2,1,0:T(8,128)} %param.11) | copy-start | bytes 12292
  152.5 125.0 %copy-start.3 = (f32[16,64]{1,0:T(8,128)S(1)}, f32[16,64]{1,0:T(8,128)}, u32[]{:S(2)}) copy-start(f32[16,64]{1,0:T(8,128)} %param.12) | copy-start | bytes 12292
Sparse Core Ops, SparseCore 0:
  86.0 60.7 all-gather.3
  152.7 90.6 reduce-scatter.1
where the time goes:
time: 325 us; the launch traced here: 324 us
  waiting for transfers between devices  151 us (46%)
  blocking collectives  141 us (43%)
  between operations  17.9 us (6%)
  matrix products  9.69 us (3%)
    reduce_scatter x1, waiting for transfers between devices, local(): lax.psum_scatter(jnp.dot(act, w_down, preferred_element_type=jnp.float32)...  90.1 us
    unnamed x1, blocking collectives  72.1 us
    all_gather x1, waiting for transfers between devices, local(): lax.all_gather(normed, 'tp', axis=0, tiled=True)  60.8 us
    psum x1, blocking collectives, local(): total = lax.psum(local_sum, 'tp')  37 us
    all_gather x1, blocking collectives, prefix(): pieces = lax.all_gather(value, axis)  31.7 us
  transfers between devices with their start and end apart: 2, of which 2 were waited for; matrix products, arithmetic and copies ran while one was open for 0% of the time, Pallas kernels for 0%

commit v1 on v0

v1 whole, which is shorter than its diff:
```python
import jax
import jax.numpy as jnp
from jax import lax
from jax.sharding import PartitionSpec as P


def spread(value, axis):
    count = lax.axis_size(axis)
    copies = lax.optimization_barrier(jnp.broadcast_to(value[None], (count,) + value.shape))
    return lax.all_to_all(copies, axis, 0, 0, tiled=True)


def layer_norm(hidden, scale, shift):
    center = hidden - jnp.mean(hidden, axis=-1, keepdims=True)
    spread = jnp.mean(center * center, axis=-1, keepdims=True)
    return (center / jnp.sqrt(spread + 1e-06) * (1.0 + scale) + shift).astype(jnp.bfloat16)


def local(latents, start_latent, t_index, dt_units, w_time, w_in, w_up, w_down, w_out):
    width = w_in.shape[1]
    tok_rows = latents.shape[1]
    channels = latents.shape[2]
    half = w_time.shape[0] // 2
    devices = lax.axis_size("tp")
    freqs = jnp.exp(-jnp.log(10000.0) * jnp.arange(half).astype(jnp.float32) / half)
    angle = t_index.astype(jnp.float32)[:, None] * freqs[None, :]
    emb = jnp.concatenate([jnp.cos(angle), jnp.sin(angle)], axis=1).astype(jnp.bfloat16)
    mod_part = jnp.dot(emb, w_time, preferred_element_type=jnp.float32)
    sent = jnp.concatenate([mod_part.reshape(-1), latents.reshape(-1)])
    got = spread(sent, "tp")
    share = mod_part.shape[1]
    mods = got[:, :share].reshape(1, -1)
    rows = got[:, share:].reshape(devices * tok_rows, channels).astype(jnp.bfloat16)
    shift = mods[:, :width]
    scale = mods[:, width : 2 * width]
    gate = mods[:, 2 * width :]
    hidden = jnp.dot(rows, w_in, preferred_element_type=jnp.float32)
    normed = layer_norm(hidden, scale, shift)
    act = jax.nn.gelu(
        jnp.dot(normed, w_up, preferred_element_type=jnp.float32), approximate=True
    ).astype(jnp.bfloat16)
    out_full = w_out.astype(jnp.float32)
    branch = gate * jnp.dot(act, w_down, preferred_element_type=jnp.float32)
    partial = jnp.dot(branch, out_full, precision=lax.Precision.HIGHEST)
    parts = lax.all_to_all(partial.reshape(devices, tok_rows, channels), "tp", 0, 0, tiled=True)
    own = jnp.dot(latents[0].astype(jnp.bfloat16), w_in, preferred_element_type=jnp.float32)
    drift = jnp.dot(own, out_full, precision=lax.Precision.HIGHEST) + jnp.sum(parts, axis=0)
    weighted = (dt_units.astype(jnp.float32) * 0.0078125)[:, None] * drift
    steps = spread(weighted, "tm")
    earlier = lax.iota(jnp.int32, steps.shape[0]) < lax.axis_index("tm")
    before = jnp.sum(jnp.where(earlier[:, None, None], steps, 0.0), axis=0)
    new_latents = (start_latent + before)[None]
    change = new_latents - latents
    local_sum = jnp.broadcast_to(jnp.sum(change * change), (1, 128))
    total = jnp.sum(spread(local_sum, "tp")[:, 0, 0])
    step_error = (total / (tok_rows * devices * channels)).reshape(1)
    return (new_latents, step_error)


def solution(mesh):
    in_specs = (
        P("tm", "tp", None),
        P("tp", None),
        P("tm"),
        P("tm"),
        P(None, "tp"),
        P(),
        P(None, "tp"),
        P("tp", None),
        P(),
    )
    out_specs = (P("tm", "tp", None), P("tm"))
    return jax.shard_map(local, mesh=mesh, in_specs=in_specs, out_specs=out_specs, check_vma=False)
```

time: 325 us -> 95.2 us (0.29)
  waiting for transfers between devices: 151 us -> 22.7 us
  blocking collectives: 141 us -> 25.6 us
  starting transfers between devices: 0.08 us -> 19.1 us
  between operations: 17.9 us -> 4.06 us
  local copies, waits for them, and re-layouts: 1.6 us -> 5.78 us
  matrix products: 9.69 us -> 13.2 us
    reduce_scatter x1 -> x0, waiting for transfers between devices: 90.1 us -> none  [local(): lax.psum_scatter(jnp.dot(act, w_down, preferred_element_type=jnp.float32)...]
    unnamed x1 -> x0, blocking collectives: 72.1 us -> none
    all_gather x1 -> x0, waiting for transfers between devices: 60.8 us -> none  [local(): lax.all_gather(normed, 'tp', axis=0, tiled=True)]
    psum x1 -> x0, blocking collectives: 37 us -> none  [local(): total = lax.psum(local_sum, 'tp')]
    all_gather x1 -> x0, blocking collectives: 31.7 us -> none  [prefix(): pieces = lax.all_gather(value, axis)]
    all_to_all x0 -> x2, blocking collectives: none -> 25.6 us  [spread(): return lax.all_to_all(copies, axis, 0, 0, tiled=True)]
    all_to_all x0 -> x2, waiting for transfers between devices: none -> 22.7 us  [the longest x1 17.2 us: spread(): return lax.all_to_all(copies, axis, 0, 0, tiled=True)]
    all_to_all x0 -> x2, starting transfers between devices: none -> 19.1 us  [the longest x1 14.4 us: spread(): return lax.all_to_all(copies, axis, 0, 0, tiled=True)]
where the time goes in v1:
time: 95.2 us; the launch traced here: 94.8 us
  blocking collectives  25.6 us (27%)
  waiting for transfers between devices  22.7 us (24%)
  starting transfers between devices  19.1 us (20%)
  matrix products  13.2 us (14%)
  local copies, waits for them, and re-layouts  5.78 us (6%)
  other arithmetic  4.32 us (5%)
  between operations  4.06 us (4%)
    all_to_all x2, blocking collectives, spread(): return lax.all_to_all(copies, axis, 0, 0, tiled=True)  25.6 us
    all_to_all x1, waiting for transfers between devices, spread(): return lax.all_to_all(copies, axis, 0, 0, tiled=True)  17.2 us
    all_to_all x1, starting transfers between devices, spread(): return lax.all_to_all(copies, axis, 0, 0, tiled=True)  14.4 us
    dot_general x1, matrix products, local(): branch = gate * jnp.dot(act, w_down, preferred_element_type=jnp.float32)  6.39 us
    all_to_all x1, waiting for transfers between devices, local(): lax.all_to_all(partial.reshape(devices, tok_rows, channels), 'tp', 0, 0,...  5.52 us
    all_to_all x1, starting transfers between devices, local(): lax.all_to_all(partial.reshape(devices, tok_rows, channels), 'tp', 0, 0,...  4.74 us
    unnamed x17, local copies, waits for them, and re-layouts  3.44 us
    dot_general x1, matrix products, local(): partial = jnp.dot(branch, out_full, precision=lax.Precision.HIGHEST)  3.43 us
  transfers between devices with their start and end apart: 2, of which 2 were waited for; matrix products, arithmetic and copies ran while one was open for 0% of the time, Pallas kernels for 0%

profile of v1, /device:TPU:2, one launch (start us, length us, event | category | flops | bytes accessed | tf_op | source)
XLA Modules:
  0.0 94.8 jit_solution(573204631701936948)
XLA Ops:
  0.6 0.0 copy-start
  1.5 0.8 reshape.61
  2.3 1.2 %convolution_reduce_fusion = f32[576]{0:T(1024)S(1)} fusion(bf16[256,1]{0,1:T(2,128)(2,1)S(1)} %reshape.65, bf16[256,576]{0,1:T(8,128)(2,1)} %param.13), kind=kOutput, calls=%fused_computation.6 | convolution fusion | flops 294912 | bytes 297728 | tf_op jit(solution)/shard_map/dot_general | solution.py:28
  3.5 0.1 pad_maximum_fusion
  3.5 0.1 all_to_all.17
  3.6 14.9 %all_to_all.27 = f32[16,1,1600]{2,1,0:T(1,128)S(1)} all-to-all(f32[16,1,1600]{2,1,0:T(1,128)S(1)} %all_to_all.17), channel_id=1, replica_groups=mesh['tm'=32,'tp'=16] {'tp'}, dimensions={0} | all-to-all | bytes 204800 | tf_op jit(solution)/shard_map/all_to_all | solution.py:10
  18.5 0.1 slice.34
  18.6 0.1 convert_element_type.39
  18.7 1.6 %fusion.21 = (f32[256]{0:T(256)S(1)}, f32[256,3072]{1,0:T(8,128)S(1)}) fusion(bf16[256,64]{1,0:T(8,128)(2,1)S(1)} %convert_element_type.39, bf16[64,3072]{1,0:T(8,128)(2,1)} %param.14), kind=kOutput, calls=%fused_computation.42 | convolution fusion | flops 101449472 | bytes 3572736 | tf_op jit(solution)/shard_map/dot_general | solution.py:37
  20.4 0.0 copy-start.1
  20.4 1.7 %copy-done.1 = f32[256,3072]{1,0:T(8,128)} copy-done((f32[256,3072]{1,0:T(8,128)}, f32[256,3072]{1,0:T(8,128)S(1)}, u32[]{:S(2)}) %copy-start.1) | copy-done | bytes 3145752
  22.0 0.5 multiply_reduce_fusion
  22.5 0.1 reshape.62
  22.6 0.0 copy-done
  22.6 0.0 copy-start.2
  22.6 6.4 %convolution_multiply_fusion = f32[256,3072]{1,0:T(8,128)} fusion(bf16[384,3072]{1,0:T(8,128)(2,1)S(1)} %copy-done, f32[3072]{0:T(1024)S(1)} %bitcast.32, bf16[3072,384]{1,0:T(8,128)(2,1)} %param.15, f32[256,3072]{1,0:T(8,128)} %copy-done.1, f32[3072]{0:T(1024)S(1)} %bitcast.31, f32[3072]{0:T(1024)S(1)} %bitcast.30, f32[256]{0:T(256)S(1)} %add_sqrt_fusion, ...), kind=kOutput, calls=%fused_computation | convolution fusion | flops 1213562880 | bytes 11048960 | tf_op jit(solution)/shard_map/dot_general | solution.py:43
  29.0 0.0 copy-done.2
  29.0 0.0 copy-start.3
  29.0 0.0 copy-start.4
  29.0 0.0 copy-start.5
  29.1 3.4 %fusion.22 = f32[256,64]{1,0:T(8,128)S(1)} fusion(f32[256,3072]{1,0:T(8,128)} %convolution_multiply_fusion, bf16[3072,64]{0,1:T(8,128)(2,1)S(1)} %copy-done.2), kind=kOutput, calls=%fused_computation.43 | convolution fusion | flops 603979776 | bytes 3604480 | tf_op jit(solution)/shard_map/dot_general | solution.py:44
  32.5 0.7 reshape.68
  33.2 4.7 %all-to-all-start.1 = ((f32[16,1,1024]{2,1,0:T(1,128)}), f32[16,1,1024]{2,1,0:T(1,128)S(1)}, u32[]{:S(2)}, u32[]{:S(2)}) async-start(f32[16,1,1024]{2,1,0:T(1,128)} %reshape.68), calls=%async_computation.1 | async-start | bytes 131072 | tf_op jit(solution)/shard_map/all_to_all | solution.py:45
  38.0 0.0 copy-done.3
  38.0 0.0 copy-done.4
  38.0 0.2 fusion.14
  38.8 5.5 %all-to-all-done.1 = f32[16,1,1024]{2,1,0:T(1,128)S(1)} async-done(((f32[16,1,1024]{2,1,0:T(1,128)}), f32[16,1,1024]{2,1,0:T(1,128)S(1)}, u32[]{:S(2)}, u32[]{:S(2)}) %all-to-all-start.1) | async-done | bytes 65568 | tf_op jit(solution)/shard_map/all_to_all | solution.py:45
  44.3 0.5 broadcast.47
  44.9 0.8 reduce.3
  45.7 0.1 reshape.69
  45.8 0.4 fusion.1
  46.2 0.8 reshape.70
  47.1 14.4 %all-to-all-start.2 = ((f32[32,1,1024]{2,1,0:T(1,128)}), f32[32,1,1024]{2,1,0:T(1,128)S(1)}, u32[]{:S(2)}, u32[]{:S(2)}) async-start(f32[32,1,1024]{2,1,0:T(1,128)} %reshape.70), calls=%async_computation.2 | async-start | bytes 262144 | tf_op jit(solution)/shard_map/all_to_all | solution.py:10
  61.4 17.2 %all-to-all-done.2 = f32[32,1,1024]{2,1,0:T(1,128)S(1)} async-done(((f32[32,1,1024]{2,1,0:T(1,128)}), f32[32,1,1024]{2,1,0:T(1,128)S(1)}, u32[]{:S(2)}, u32[]{:S(2)}) %all-to-all-start.2) | async-done | bytes 131104 | tf_op jit(solution)/shard_map/all_to_all | solution.py:10
  78.7 1.0 %reduce.4 = f32[32,1024]{1,0:T(8,128)S(1)} reduce(f32[32,1,1024]{2,1,0:T(1,128)S(1)} %all-to-all-done.2, f32[]{:T(128)} %broadcast.47), dimensions={1}, to_apply=%all_to_all.21.reduce_sub_computation | reduce | bytes 262148 | tf_op jit(solution)/shard_map/all_to_all | solution.py:10
  79.6 0.1 reshape.71
  79.7 0.1 select_reduce_fusion
  79.8 0.0 copy-done.5
  79.8 1.2 %multiply_reduce_fusion.1 = (f32[]{:T(128)}, f32[1,16,64]{2,1,0:T(8,128)}) fusion(f32[1,16,64]{2,1,0:T(8,128)S(1)} %copy-done.4, f32[16,64]{1,0:T(8,128)S(1)} %copy-done.5, f32[16,64]{1,0:T(8,128)S(1)} %select_reduce_fusion), kind=kLoop, calls=%fused_computation.26 | loop fusion | flops 4095 | bytes 16388 | tf_op jit(solution)/shard_map/reduce_sum | solution.py:54
  81.0 0.6 broadcast_in_dim_broadcast_in_dim_broadcast_in_dim.3
  81.7 10.7 %all_to_all.28 = f32[16,1,128]{2,1,0:T(1,128)S(1)} all-to-all(f32[16,1,128]{2,1,0:T(1,128)S(1)} %broadcast_in_dim_broadcast_in_dim_broadcast_in_dim.3), channel_id=1, replica_groups=mesh['tm'=32,'tp'=16] {'tp'}, dimensions={0} | all-to-all | bytes 16384 | tf_op jit(solution)/shard_map/all_to_all | solution.py:10
  92.4 0.6 slice_reduce_fusion
  (12 shorter events, 0.2 us)
Async XLA Ops:
  0.6 22.0 %copy-start = (bf16[384,3072]{1,0:T(8,128)(2,1)S(1)}, bf16[384,3072]{1,0:T(8,128)(2,1)}, u32[]{:S(2)}) copy-start(bf16[384,3072]{1,0:T(8,128)(2,1)} %param.16) | copy-start | bytes 7077892
  20.4 1.7 %copy-start.1 = (f32[256,3072]{1,0:T(8,128)}, f32[256,3072]{1,0:T(8,128)S(1)}, u32[]{:S(2)}) copy-start(f32[256,3072]{1,0:T(8,128)S(1)} %get-tuple-element.8) | copy-start | bytes 9437188
  22.6 6.4 %copy-start.2 = (bf16[3072,64]{0,1:T(8,128)(2,1)S(1)}, bf16[3072,64]{0,1:T(8,128)(2,1)}, u32[]{:S(2)}) copy-start(bf16[3072,64]{0,1:T(8,128)(2,1)} %param.17) | copy-start | bytes 1179652
  29.0 8.9 %copy-start.3 = (bf16[64,3072]{1,0:T(8,128)(2,1)S(1)}, bf16[64,3072]{1,0:T(8,128)(2,1)}, u32[]{:S(2)}) copy-start(bf16[64,3072]{1,0:T(8,128)(2,1)} %param.14) | copy-start | bytes 1179652
  29.0 8.9 %copy-start.4 = (f32[1,16,64]{2,1,0:T(8,128)S(1)}, f32[1,16,64]{2,1,0:T(8,128)}, u32[]{:S(2)}) copy-start(f32[1,16,64]{2,1,0:T(8,128)} %param.9) | copy-start | bytes 12292
  29.0 50.8 %copy-start.5 = (f32[16,64]{1,0:T(8,128)S(1)}, f32[16,64]{1,0:T(8,128)}, u32[]{:S(2)}) copy-start(f32[16,64]{1,0:T(8,128)} %param.10) | copy-start | bytes 12292
  33.2 11.1 %all-to-all-start.1 = ((f32[16,1,1024]{2,1,0:T(1,128)}), f32[16,1,1024]{2,1,0:T(1,128)S(1)}, u32[]{:S(2)}, u32[]{:S(2)}) async-start(f32[16,1,1024]{2,1,0:T(1,128)} %reshape.68), calls=%async_computation.1 | async-start | bytes 131072 | tf_op jit(solution)/shard_map/all_to_all | solution.py:45
  47.1 31.6 %all-to-all-start.2 = ((f32[32,1,1024]{2,1,0:T(1,128)}), f32[32,1,1024]{2,1,0:T(1,128)S(1)}, u32[]{:S(2)}, u32[]{:S(2)}) async-start(f32[32,1,1024]{2,1,0:T(1,128)} %reshape.70), calls=%async_computation.2 | async-start | bytes 262144 | tf_op jit(solution)/shard_map/all_to_all | solution.py:10

commit v2 on v1

v2 whole, which is shorter than its diff:
```python
import functools

import jax
import jax.numpy as jnp
from jax import lax
from jax.experimental import pallas as pl
from jax.experimental.pallas import tpu as pltpu
from jax.sharding import Mesh
from jax.sharding import PartitionSpec as P

LANES = 128
MODS_AT = 8
VMEM = pl.BlockSpec(memory_space=pltpu.VMEM)
SMEM = pl.BlockSpec(memory_space=pltpu.SMEM)
F32 = jnp.float32
BF16 = jnp.bfloat16


def call(body, out_shape, in_specs, name, flops=0, scratch=()):
    return pl.pallas_call(
        body,
        out_shape=out_shape,
        in_specs=in_specs,
        out_specs=jax.tree.map(lambda _: VMEM, out_shape),
        scratch_shapes=list(scratch),
        cost_estimate=pl.CostEstimate(flops=flops, bytes_accessed=1 << 20, transcendentals=0),
        compiler_params=pltpu.CompilerParams(vmem_limit_bytes=48 << 20),
        name=name,
    )


def fold(rows):
    half = rows.shape[0] // 2
    return jnp.concatenate([rows[:half], rows[half:]], axis=1)


def swap(value):
    return pltpu.roll(value, value.shape[-1] // 2, value.ndim - 1)


def left(shape):
    return lax.broadcasted_iota(jnp.int32, shape, len(shape) - 1) < shape[-1] // 2


def split(value):
    high = value.astype(BF16).astype(F32)
    return high, value - high


def prepare(place, t_index, latents, w_time, sent):
    half = w_time.shape[1] // 2
    order = lax.broadcasted_iota(jnp.int32, (16, half), 1).astype(F32)
    freqs = jnp.exp(-jnp.log(jnp.full((16, half), 10000.0, F32)) * order / half)
    angle = jnp.full((16, half), t_index[0], jnp.int32).astype(F32) * freqs
    emb = jnp.concatenate([jnp.cos(angle), jnp.sin(angle)], axis=1).astype(BF16)
    dims = (((1,), (1,)), ((), ()))
    mods = lax.dot_general(emb, w_time[...], dims, preferred_element_type=F32)[:1]
    gap = jnp.zeros((1, LANES // 2), F32)
    odd = place[0] % 2 == 1
    mods = jnp.where(odd, jnp.concatenate([gap, mods], 1), jnp.concatenate([mods, gap], 1))
    lines = mods.shape[1] // LANES
    rows = [fold(latents[0])] + [mods[:, i * LANES : (i + 1) * LANES] for i in range(lines)]
    rows.append(jnp.zeros((16 - MODS_AT - lines, LANES), F32))
    block = jnp.concatenate(rows, axis=0)
    for device in range(sent.shape[0]):
        sent[device] = block


def own_part(dt_units, latents, w_in, w_out_t, own):
    rows = latents[0].astype(BF16)
    hidden = jnp.dot(rows, w_in[...], preferred_element_type=F32)
    high, low = split(hidden)
    rest, last = split(low)
    stacked = jnp.concatenate([high, rest, last], axis=0).astype(BF16)
    dims = (((1,), (1,)), ((), ()))
    out = lax.dot_general(stacked, w_out_t[...], dims, preferred_element_type=F32)
    drift = out[:16] + out[16:32] + out[32:48]
    own[...] = fold(drift * (dt_units[0].astype(F32) * 0.0078125))


def block(place, dt_units, got, own, w_in, w_up, w_down, w_out_t, sent, hidden, normed):
    devices = got.shape[0]
    width = w_in.shape[1]
    count = width // LANES
    pairs = []
    for device in range(0, devices, 2):
        even = [got[device, MODS_AT + i : MODS_AT + i + 1, :] for i in range(5)]
        odd = [got[device + 1, MODS_AT + i : MODS_AT + i + 1, :] for i in range(5)]
        pairs += even[:4] + [even[4] + odd[0]] + odd[1:]
    shift, scale, gate = pairs[:count], pairs[count : 2 * count], pairs[2 * count :]
    dims = (((1,), (1,)), ((), ()))
    gated = w_out_t[...].astype(F32) * jnp.concatenate(gate, axis=1)
    high, low = split(gated)
    gated = jnp.concatenate([high, low], axis=0).astype(BF16)
    down = lax.dot_general(w_down[...], gated, dims, preferred_element_type=F32)
    down = down + swap(down)
    high, low = split(down)
    down = jnp.where(left(down.shape), high, low).astype(BF16)

    lat = got[:, :MODS_AT, :].reshape(devices * MODS_AT, LANES)
    lat = jnp.concatenate([lat[:, : LANES // 2], lat[:, LANES // 2 :]], axis=0).astype(BF16)
    tokens = lat.shape[0]
    step = 512
    total = jnp.zeros((tokens, LANES), F32)
    for start in range(0, width, step):
        part = jnp.dot(lat, w_in[:, start : start + step], preferred_element_type=F32)
        hidden[:, start : start + step] = part
        for at in range(0, step, LANES):
            total = total + part[:, at : at + LANES]
    mean = jnp.sum(total, axis=1, keepdims=True) / width
    total = jnp.zeros((tokens, LANES), F32)
    for start in range(0, width, LANES):
        center = hidden[:, start : start + LANES] - mean
        total = total + center * center
    spread = jnp.sum(total, axis=1, keepdims=True) / width
    inverse = 1.0 / jnp.sqrt(spread + 1e-06)
    for i in range(count):
        at = slice(i * LANES, (i + 1) * LANES)
        value = (hidden[:, at] - mean) * inverse * (1.0 + scale[i]) + shift[i]
        normed[:, at] = value.astype(BF16)
    up = jnp.dot(normed[...], w_up[...], preferred_element_type=F32)
    act = jax.nn.gelu(up, approximate=True).astype(BF16)
    part = jnp.dot(act, down, preferred_element_type=F32)
    part = part + swap(part)
    half = tokens // 2
    part = jnp.where(left((half, LANES)), part[:half], part[half:])
    part = part * (dt_units[0].astype(F32) * 0.0078125)
    part = part.reshape(devices, MODS_AT, LANES)
    mine = lax.broadcasted_iota(jnp.int32, part.shape, 0) == place[0]
    part = jnp.where(mine, part + own[...][None], part)
    sent[0] = part
    sent[1] = part


def combine(parts, sent, first):
    one = parts[0, 0]
    two = parts[1, 0]
    for device in range(1, parts.shape[1]):
        one = one + parts[0, device]
        two = two + parts[1, device]
    first[...] = one
    both = (one + two).astype(BF16)
    for device in range(sent.shape[0]):
        sent[device] = both


def finish(place, steps, first, start_latent, latents, new_latents, sent):
    before = jnp.where(place[2] == 1, first[...], 0.0)
    for z in range(steps.shape[0]):
        before = before + jnp.where(z < place[1], steps[z].astype(F32), 0.0)
    half = LANES // 2
    before = jnp.concatenate([before[:, :half], before[:, half:]], axis=0)
    value = start_latent[...] + before
    new_latents[0] = value
    change = value - latents[0]
    total = jnp.sum(change * change)
    sent[...] = jnp.full(sent.shape, total, F32)


def local(latents, start_latent, t_index, dt_units, w_time, w_in, w_up, w_down, w_out):
    zs, devices = lax.axis_size("z"), lax.axis_size("tp")
    tok_rows, channels = latents.shape[1:]
    width = w_in.shape[1]
    hid = w_up.shape[1]
    tokens = tok_rows * devices
    place = jnp.stack([lax.axis_index("tp"), lax.axis_index("z"), lax.axis_index("core")])
    w_out_t = w_out.T

    sent = call(
        prepare,
        jax.ShapeDtypeStruct((devices, 16, LANES), F32),
        [SMEM, SMEM, VMEM, VMEM],
        "prepare",
    )(place, t_index, latents, w_time.T)
    got = lax.all_to_all(sent, "tp", 0, 0, tiled=True)
    own = call(
        own_part,
        jax.ShapeDtypeStruct((MODS_AT, LANES), F32),
        [SMEM, VMEM, VMEM, VMEM],
        "own_part",
        flops=4 * tok_rows * width * channels,
    )(dt_units, latents, w_in, w_out_t)
    sent = call(
        block,
        jax.ShapeDtypeStruct((2, devices, MODS_AT, LANES), F32),
        [SMEM, SMEM] + [VMEM] * 6,
        "block",
        flops=2 * tokens * width * (hid + channels) + 2 * hid * width * channels,
        scratch=[pltpu.VMEM((tokens, width), F32), pltpu.VMEM((tokens, width), BF16)],
    )(place, dt_units, got, own, w_in, w_up, w_down, w_out_t)
    sent = sent.reshape(2 * devices, MODS_AT, LANES)
    parts = lax.all_to_all(sent, ("core", "tp"), 0, 0, tiled=True)
    parts = parts.reshape(2, devices, MODS_AT, LANES)
    sent, first = call(
        combine,
        (
            jax.ShapeDtypeStruct((zs, MODS_AT, LANES), BF16),
            jax.ShapeDtypeStruct((MODS_AT, LANES), F32),
        ),
        [VMEM],
        "combine",
    )(parts)
    steps = lax.all_to_all(sent, "z", 0, 0, tiled=True)
    new_latents, sent = call(
        finish,
        (
            jax.ShapeDtypeStruct(latents.shape, F32),
            jax.ShapeDtypeStruct((devices, 1, LANES), F32),
        ),
        [SMEM, VMEM, VMEM, VMEM, VMEM],
        "finish",
    )(place, steps, first, start_latent, latents)
    totals = lax.all_to_all(sent, "tp", 0, 0, tiled=True)
    step_error = (jnp.sum(totals[:, 0, 0]) / (tokens * channels)).reshape(1)
    return (new_latents, step_error)


def solution(mesh):
    tm, tp = (mesh.shape["tm"], mesh.shape["tp"])
    grid = Mesh(mesh.devices.reshape(tm // 2, 2, tp), ("z", "core", "tp"))
    steps = ("z", "core")
    in_specs = (
        P(steps, "tp", None),
        P("tp", None),
        P(steps),
        P(steps),
        P(None, "tp"),
        P(),
        P(None, "tp"),
        P("tp", None),
        P(),
    )
    out_specs = (P(steps, "tp", None), P(steps))
    return jax.shard_map(local, mesh=grid, in_specs=in_specs, out_specs=out_specs, check_vma=False)
```

time: 95.2 us -> 81.1 us (0.85)
  blocking collectives: 25.6 us -> 47.6 us
  waiting for transfers between devices: 22.7 us -> 2.96 us
  matrix products: 13.2 us -> 0 us
  starting transfers between devices: 19.1 us -> 9.21 us
  Pallas kernels: 0 us -> 6.65 us
  local copies, waits for them, and re-layouts: 5.78 us -> 9.67 us
  other arithmetic: 4.32 us -> 0.69 us
    all_to_all x2 -> x3, blocking collectives: 25.6 us -> 47.6 us  [the longest x1 25.7 us: local(): steps = lax.all_to_all(sent, 'z', 0, 0, tiled=True)]
    all_to_all x2 -> x1, waiting for transfers between devices: 22.7 us -> 2.96 us  [local(): got = lax.all_to_all(sent, 'tp', 0, 0, tiled=True)]
    dot_general x6 -> x0, matrix products: 13.2 us -> none  [the longest x1 6.39 us: local(): branch = gate * jnp.dot(act, w_down, preferred_element_type=jnp.float32)]
    all_to_all x2 -> x1, starting transfers between devices: 19.1 us -> 9.21 us  [local(): got = lax.all_to_all(sent, 'tp', 0, 0, tiled=True)]
    pallas_call x0 -> x5, Pallas kernels: none -> 6.65 us  [the longest x1 3.52 us: local(): call(block, jax.ShapeDtypeStruct((2, devices, MODS_AT, LANES), F32), [SME...]
    unnamed x17 -> x22, local copies, waits for them, and re-layouts: 3.44 us -> 9.67 us
    reduce_sum x5 -> x1, other arithmetic: 2.39 us -> 0.62 us  [local(): step_error = (jnp.sum(totals[:, 0, 0]) / (tokens * channels)).reshape(1)]
    all_to_all x2 -> x0, other arithmetic: 1.76 us -> none  [the longest x1 0.95 us: spread(): return lax.all_to_all(copies, axis, 0, 0, tiled=True)]
  transfers between devices with their start and end apart: 2 -> 1, of which waited for: 2 -> 1; matrix products, arithmetic and copies ran while one was open for 0% -> 0% of each run, Pallas kernels for 0% -> 1%
where the time goes in v2:
time: 81.1 us; the launch traced here: 80.5 us
  blocking collectives  47.6 us (59%)
  local copies, waits for them, and re-layouts  9.67 us (12%)
  starting transfers between devices  9.21 us (11%)
  Pallas kernels  6.65 us (8%)
  between operations  3.74 us (5%)
  waiting for transfers between devices  2.96 us (4%)
    all_to_all x1, blocking collectives, local(): steps = lax.all_to_all(sent, 'z', 0, 0, tiled=True)  25.7 us
    all_to_all x1, blocking collectives, local(): parts = lax.all_to_all(sent, ('core', 'tp'), 0, 0, tiled=True)  11.2 us
    all_to_all x1, blocking collectives, local(): totals = lax.all_to_all(sent, 'tp', 0, 0, tiled=True)  10.6 us
    unnamed x22, local copies, waits for them, and re-layouts  9.67 us
    all_to_all x1, starting transfers between devices, local(): got = lax.all_to_all(sent, 'tp', 0, 0, tiled=True)  9.21 us
    pallas_call x1, Pallas kernels, local(): call(block, jax.ShapeDtypeStruct((2, devices, MODS_AT, LANES), F32), [SME...  3.52 us
    all_to_all x1, waiting for transfers between devices, local(): got = lax.all_to_all(sent, 'tp', 0, 0, tiled=True)  2.96 us
  transfers between devices with their start and end apart: 1, of which 1 were waited for; matrix products, arithmetic and copies ran while one was open for 0% of the time, Pallas kernels for 1%

profile of v2, /device:TPU:2, one launch (start us, length us, event | category | flops | bytes accessed | tf_op | source)
XLA Modules:
  0.0 80.5 jit_solution(3718643413008041834)
XLA Ops:
  1.3 0.1 pad_add_fusion.place
  1.4 0.0 copy-start.6
  1.4 1.0 %copy-done.6 = bf16[256,576]{0,1:T(8,128)(2,1)S(1)} copy-done((bf16[256,576]{0,1:T(8,128)(2,1)S(1)}, bf16[256,576]{0,1:T(8,128)(2,1)}, u32[]{:S(2)}) %copy-start.6) | copy-done | bytes 294936
  2.3 0.0 copy-start.7
  2.3 0.7 copy-done.7
  3.0 1.5 %prepare.1 = f32[16,16,128]{2,1,0:T(8,128)} custom-call(s32[3]{0:T(128)S(1)} %pad_add_fusion.place, s32[1]{0:T(128)S(6)} %copy.11.t_index, f32[1,16,64]{2,1,0:T(8,128)S(1)} %copy-done.7, bf16[576,256]{1,0:T(8,128)(2,1)S(1)} %bitcast.12), custom_call_target="tpu_custom_call" | custom-call | bytes 1048576 | tf_op jit(solution)/shard_map/prepare/pallas_call | solution.py:169
  4.5 9.2 %all-to-all-start = ((f32[16,16,128]{2,1,0:T(8,128)}), f32[16,16,128]{2,1,0:T(8,128)S(1)}, u32[]{:S(2)}, u32[]{:S(2)}) async-start(f32[16,16,128]{2,1,0:T(8,128)} %prepare.1), calls=%async_computation | async-start | bytes 262144 | tf_op jit(solution)/shard_map/all_to_all | solution.py:175
  14.3 0.0 copy-start.2
  14.3 1.0 %copy-done.2 = bf16[64,3072]{1,0:T(8,128)(2,1)S(1)} copy-done((bf16[64,3072]{1,0:T(8,128)(2,1)S(1)}, bf16[64,3072]{1,0:T(8,128)(2,1)}, u32[]{:S(2)}) %copy-start.2) | copy-done | bytes 393240
  15.3 0.0 copy-start.4
  15.3 1.0 %copy-done.4 = bf16[3072,64]{0,1:T(8,128)(2,1)S(1)} copy-done((bf16[3072,64]{0,1:T(8,128)(2,1)S(1)}, bf16[3072,64]{0,1:T(8,128)(2,1)}, u32[]{:S(2)}) %copy-start.4) | copy-done | bytes 393240
  16.3 0.0 copy-start.8
  16.3 0.7 copy-done.8
  17.0 0.4 own_part.1.own
  17.4 3.0 %all-to-all-done.got = f32[16,16,128]{2,1,0:T(8,128)S(1)} async-done(((f32[16,16,128]{2,1,0:T(8,128)}), f32[16,16,128]{2,1,0:T(8,128)S(1)}, u32[]{:S(2)}, u32[]{:S(2)}) %all-to-all-start) | async-done | bytes 131104 | tf_op jit(solution)/shard_map/all_to_all | solution.py:175
  20.4 0.0 copy-start
  20.4 1.7 %copy-done = bf16[3072,384]{1,0:T(8,128)(2,1)S(1)} copy-done((bf16[3072,384]{1,0:T(8,128)(2,1)S(1)}, bf16[3072,384]{1,0:T(8,128)(2,1)}, u32[]{:S(2)}) %copy-start) | copy-done | bytes 2359320
  22.1 0.0 copy-start.1
  22.1 1.7 %copy-done.1 = bf16[384,3072]{1,0:T(8,128)(2,1)S(1)} copy-done((bf16[384,3072]{1,0:T(8,128)(2,1)S(1)}, bf16[384,3072]{1,0:T(8,128)(2,1)}, u32[]{:S(2)}) %copy-start.1) | copy-done | bytes 2359320
  23.7 0.0 copy-start.3
  23.7 1.0 %copy-done.3 = bf16[64,3072]{1,0:T(8,128)(2,1)S(1)} copy-done((bf16[64,3072]{1,0:T(8,128)(2,1)S(1)}, bf16[64,3072]{1,0:T(8,128)(2,1)}, u32[]{:S(2)}) %copy-start.3) | copy-done | bytes 393240
  24.7 0.0 copy-start.5
  24.7 1.0 %copy-done.5 = bf16[3072,64]{0,1:T(8,128)(2,1)S(1)} copy-done((bf16[3072,64]{0,1:T(8,128)(2,1)S(1)}, bf16[3072,64]{0,1:T(8,128)(2,1)}, u32[]{:S(2)}) %copy-start.5) | copy-done | bytes 393240
  25.7 0.0 copy-start.9
  25.7 0.0 copy-start.10
  25.7 3.5 %block.1 = f32[2,16,8,128]{3,2,1,0:T(8,128)S(1)} custom-call(s32[3]{0:T(128)S(1)} %pad_add_fusion.place, s32[1]{0:T(128)S(6)} %copy.12.dt_units, f32[16,16,128]{2,1,0:T(8,128)S(1)} %all-to-all-done.got, f32[8,128]{1,0:T(8,128)S(1)} %own_part.1.own, bf16[64,3072]{1,0:T(8,128)(2,1)S(1)} %copy-done.3, bf16[3072,384]{1,0:T(8,128)(2,1)S(1)} %copy-done, ...), custom_call_target="tpu_custom_call" | custom-call | flops 855638016 | bytes 1048576 | tf_op jit(solution)/shard_map/block/pallas_call | solution.py:183
  29.3 11.2 %all_to_all.20 = f32[32,8,128]{2,1,0:T(8,128)S(1)} all-to-all(f32[32,8,128]{2,1,0:T(8,128)S(1)} %bitcast.10), channel_id=1, replica_groups=mesh['z'=16,'core'=2,'tp'=16] {'core','tp'}, dimensions={0} | all-to-all | bytes 262144 | tf_op jit(solution)/shard_map/all_to_all | solution.py:192
  40.5 25.7 %all_to_all.21.steps = bf16[16,8,128]{2,1,0:T(8,128)(2,1)S(1)} all-to-all(bf16[16,8,128]{2,1,0:T(8,128)(2,1)S(1)} %get-tuple-element.6), channel_id=1, replica_groups=mesh['z'=16,'core'=2,'tp'=16] {'z'}, dimensions={0} | all-to-all | bytes 65536 | tf_op jit(solution)/shard_map/all_to_all | solution.py:203
  66.2 0.0 copy-done.9
  66.2 0.0 copy-done.10
  66.2 1.2 %finish.1 = (f32[1,16,64]{2,1,0:T(8,128)}, f32[16,1,128]{2,1,0:T(1,128)S(1)}) custom-call(s32[3]{0:T(128)S(1)} %pad_add_fusion.place, bf16[16,8,128]{2,1,0:T(8,128)(2,1)S(1)} %all_to_all.21.steps, f32[8,128]{1,0:T(8,128)S(1)} %get-tuple-element.7.first, f32[16,64]{1,0:T(8,128)S(1)} %copy-done.10, f32[1,16,64]{2,1,0:T(8,128)S(1)} %copy-done.9), custom_call_target="tpu_custom_call" | custom-call | bytes 1048576 | tf_op jit(solution)/shard_map/finish/pallas_call | solution.py:204
  67.4 10.6 %all_to_all.22 = f32[16,1,128]{2,1,0:T(1,128)S(1)} all-to-all(f32[16,1,128]{2,1,0:T(1,128)S(1)} %get-tuple-element.9), channel_id=1, replica_groups=mesh['z'=16,'core'=2,'tp'=16] {'tp'}, dimensions={0} | all-to-all | bytes 16384 | tf_op jit(solution)/shard_map/all_to_all | solution.py:213
  78.1 0.6 slice_reduce_fusion
  (1 shorter events, 0.0 us)
Async XLA Ops:
  1.4 1.0 %copy-start.6 = (bf16[256,576]{0,1:T(8,128)(2,1)S(1)}, bf16[256,576]{0,1:T(8,128)(2,1)}, u32[]{:S(2)}) copy-start(bf16[256,576]{0,1:T(8,128)(2,1)} %param.13) | copy-start | bytes 884740
  2.3 0.7 copy-start.7
  4.5 15.9 %all-to-all-start = ((f32[16,16,128]{2,1,0:T(8,128)}), f32[16,16,128]{2,1,0:T(8,128)S(1)}, u32[]{:S(2)}, u32[]{:S(2)}) async-start(f32[16,16,128]{2,1,0:T(8,128)} %prepare.1), calls=%async_computation | async-start | bytes 262144 | tf_op jit(solution)/shard_map/all_to_all | solution.py:175
  14.3 1.0 %copy-start.2 = (bf16[64,3072]{1,0:T(8,128)(2,1)S(1)}, bf16[64,3072]{1,0:T(8,128)(2,1)}, u32[]{:S(2)}) copy-start(bf16[64,3072]{1,0:T(8,128)(2,1)} %w_in.3) | copy-start | bytes 1179652
  15.3 1.0 %copy-start.4 = (bf16[3072,64]{0,1:T(8,128)(2,1)S(1)}, bf16[3072,64]{0,1:T(8,128)(2,1)}, u32[]{:S(2)}) copy-start(bf16[3072,64]{0,1:T(8,128)(2,1)} %param.17) | copy-start | bytes 1179652
  16.3 0.7 copy-start.8
  20.4 1.7 %copy-start = (bf16[3072,384]{1,0:T(8,128)(2,1)S(1)}, bf16[3072,384]{1,0:T(8,128)(2,1)}, u32[]{:S(2)}) copy-start(bf16[3072,384]{1,0:T(8,128)(2,1)} %w_up.1) | copy-start | bytes 7077892
  22.1 1.7 %copy-start.1 = (bf16[384,3072]{1,0:T(8,128)(2,1)S(1)}, bf16[384,3072]{1,0:T(8,128)(2,1)}, u32[]{:S(2)}) copy-start(bf16[384,3072]{1,0:T(8,128)(2,1)} %w_down.1) | copy-start | bytes 7077892
  23.7 1.0 %copy-start.3 = (bf16[64,3072]{1,0:T(8,128)(2,1)S(1)}, bf16[64,3072]{1,0:T(8,128)(2,1)}, u32[]{:S(2)}) copy-start(bf16[64,3072]{1,0:T(8,128)(2,1)} %w_in.3) | copy-start | bytes 1179652
  24.7 1.0 %copy-start.5 = (bf16[3072,64]{0,1:T(8,128)(2,1)S(1)}, bf16[3072,64]{0,1:T(8,128)(2,1)}, u32[]{:S(2)}) copy-start(bf16[3072,64]{0,1:T(8,128)(2,1)} %param.17) | copy-start | bytes 1179652
  25.7 40.5 %copy-start.9 = (f32[1,16,64]{2,1,0:T(8,128)S(1)}, f32[1,16,64]{2,1,0:T(8,128)}, u32[]{:S(2)}) copy-start(f32[1,16,64]{2,1,0:T(8,128)} %latents.5) | copy-start | bytes 12292
  25.7 40.5 %copy-start.10 = (f32[16,64]{1,0:T(8,128)S(1)}, f32[16,64]{1,0:T(8,128)}, u32[]{:S(2)}) copy-start(f32[16,64]{1,0:T(8,128)} %start_latent.1) | copy-start | bytes 12292

commit v3 on v2

v3 whole, which is shorter than its diff:
```python
import jax
import jax.numpy as jnp
from jax import lax
from jax.experimental import pallas as pl
from jax.experimental.pallas import tpu as pltpu
from jax.sharding import Mesh
from jax.sharding import PartitionSpec as P

LANES = 128
MODS_AT = 8
SMEM = pl.BlockSpec(memory_space=pltpu.SMEM)
VMEM = pl.BlockSpec(memory_space=pltpu.VMEM)
HBM = pl.BlockSpec(memory_space=pltpu.HBM)
F32 = jnp.float32
BF16 = jnp.bfloat16


def call(body, out_shape, in_specs, name, flops=0, scratch=(), limit=16):
    return pl.pallas_call(
        body,
        out_shape=out_shape,
        in_specs=in_specs,
        out_specs=jax.tree.map(lambda _: VMEM, out_shape),
        scratch_shapes=list(scratch),
        cost_estimate=pl.CostEstimate(flops=flops, bytes_accessed=1 << 20, transcendentals=0),
        compiler_params=pltpu.CompilerParams(vmem_limit_bytes=limit << 20),
        name=name,
    )


def held(*arrays):
    return [pltpu.with_memory_space_constraint(a, pltpu.HBM) for a in arrays]


def load(pairs, sems):
    copies = [pltpu.make_async_copy(src, dst, sems.at[i]) for i, (src, dst) in enumerate(pairs)]
    for copy in copies:
        copy.start()
    return copies


def fold(rows):
    half = rows.shape[0] // 2
    return jnp.concatenate([rows[:half], rows[half:]], axis=1)


def swap(value):
    return pltpu.roll(value, value.shape[-1] // 2, value.ndim - 1)


def left(shape):
    return lax.broadcasted_iota(jnp.int32, shape, len(shape) - 1) < shape[-1] // 2


def split(value):
    high = value.astype(BF16).astype(F32)
    return high, value - high


def prepare(t_index, dt_units, latents, w_time, *refs):
    weights, (sent, factor), here = refs[:4], refs[4:6], refs[6:10]
    lat_here, w_here, sems = refs[10:]
    pairs = [(w_time, w_here), (latents, lat_here)]
    copies = load(pairs + list(zip(weights, here)), sems)
    half = w_here.shape[1] // 2
    order = lax.broadcasted_iota(jnp.int32, (16, half), 1).astype(F32)
    freqs = jnp.exp(-jnp.log(jnp.full((16, half), 10000.0, F32)) * order / half)
    angle = jnp.full((16, half), t_index[0], jnp.int32).astype(F32) * freqs
    emb = jnp.concatenate([jnp.cos(angle), jnp.sin(angle)], axis=1).astype(BF16)
    factor[...] = jnp.full(factor.shape, dt_units[0], jnp.int32).astype(F32) * 0.0078125
    copies[1].wait()
    lat = fold(lat_here[0])
    copies[0].wait()
    dims = (((1,), (1,)), ((), ()))
    mods = lax.dot_general(emb, w_here[...], dims, preferred_element_type=F32)[:1]
    gap = jnp.zeros((1, LANES // 2), F32)
    odd = lax.axis_index("tp") % 2 == 1
    mods = jnp.where(odd, jnp.concatenate([gap, mods], 1), jnp.concatenate([mods, gap], 1))
    lines = mods.shape[1] // LANES
    rows = [lat] + [mods[:, i * LANES : (i + 1) * LANES] for i in range(lines)]
    rows.append(jnp.zeros((16 - MODS_AT - lines, LANES), F32))
    block = jnp.concatenate(rows, axis=0)
    for device in range(sent.shape[0]):
        sent[device] = block
    for copy in copies[2:]:
        copy.wait()


def block(got, factor, w_in, w_out_t, w_up, w_down, sent, hidden, normed):
    devices = got.shape[0]
    width = w_in.shape[1]
    count = width // LANES
    pairs = []
    for device in range(0, devices, 2):
        even = [got[device, MODS_AT + i : MODS_AT + i + 1, :] for i in range(5)]
        odd = [got[device + 1, MODS_AT + i : MODS_AT + i + 1, :] for i in range(5)]
        pairs += even[:4] + [even[4] + odd[0]] + odd[1:]
    shift, scale, gate = pairs[:count], pairs[count : 2 * count], pairs[2 * count :]
    dims = (((1,), (1,)), ((), ()))
    gated = w_out_t[...].astype(F32) * jnp.concatenate(gate, axis=1)
    high, low = split(gated)
    gated = jnp.concatenate([high, low], axis=0).astype(BF16)
    down = lax.dot_general(w_down[...], gated, dims, preferred_element_type=F32)
    down = down + swap(down)
    high, low = split(down)
    down = jnp.where(left(down.shape), high, low).astype(BF16)

    lat = got[:, :MODS_AT, :].reshape(devices * MODS_AT, LANES)
    lat = jnp.concatenate([lat[:, : LANES // 2], lat[:, LANES // 2 :]], axis=0).astype(BF16)
    tokens = lat.shape[0]
    step = 512
    total = jnp.zeros((tokens, LANES), F32)
    for start in range(0, width, step):
        part = jnp.dot(lat, w_in[:, start : start + step], preferred_element_type=F32)
        hidden[:, start : start + step] = part
        for at in range(0, step, LANES):
            total = total + part[:, at : at + LANES]
    place = pl.multiple_of(lax.axis_index("tp") * MODS_AT, MODS_AT)
    own = [hidden[pl.ds(place + at, MODS_AT), :] for at in (0, tokens // 2)]
    high, low = split(jnp.concatenate(own, axis=0))
    rest, last = split(low)
    own = jnp.concatenate([high, rest, last], axis=0).astype(BF16)
    own = lax.dot_general(own, w_out_t[...], dims, preferred_element_type=F32)
    own = fold(own[:16] + own[16:32] + own[32:48])
    mean = jnp.sum(total, axis=1, keepdims=True) / width
    total = jnp.zeros((tokens, LANES), F32)
    for start in range(0, width, LANES):
        center = hidden[:, start : start + LANES] - mean
        total = total + center * center
    spread = jnp.sum(total, axis=1, keepdims=True) / width
    inverse = 1.0 / jnp.sqrt(spread + 1e-06)
    for i in range(count):
        at = slice(i * LANES, (i + 1) * LANES)
        value = (hidden[:, at] - mean) * inverse * (1.0 + scale[i]) + shift[i]
        normed[:, at] = value.astype(BF16)
    up = jnp.dot(normed[...], w_up[...], preferred_element_type=F32)
    act = jax.nn.gelu(up, approximate=True).astype(BF16)
    part = jnp.dot(act, down, preferred_element_type=F32)
    part = part + swap(part)
    half = tokens // 2
    part = jnp.where(left((half, LANES)), part[:half], part[half:])
    part = part.reshape(devices, MODS_AT, LANES)
    mine = lax.broadcasted_iota(jnp.int32, part.shape, 0) == lax.axis_index("tp")
    part = jnp.where(mine, part + own[None], part) * factor[...][None]
    sent[0] = part
    sent[1] = part


def combine(parts, sent, first):
    one = parts[0, 0]
    two = parts[1, 0]
    for device in range(1, parts.shape[1]):
        one = one + parts[0, device]
        two = two + parts[1, device]
    first[...] = one
    both = (one + two).astype(BF16)
    for device in range(sent.shape[0]):
        sent[device] = both


def advance(steps, first, start_latent):
    before = jnp.where(lax.axis_index("core") == 1, first[...], 0.0)
    for z in range(steps.shape[0]):
        before = before + jnp.where(z < lax.axis_index("z"), steps[z].astype(F32), 0.0)
    half = LANES // 2
    before = jnp.concatenate([before[:, :half], before[:, half:]], axis=0)
    return start_latent[...] + before


def judge(steps, first, start_latent, latents, sent):
    change = advance(steps, first, start_latent) - latents[0]
    count = change.size * sent.shape[0]
    sent[...] = jnp.full(sent.shape, jnp.sum(change * change) / count, F32)


def finish(steps, first, start_latent, new_latents):
    new_latents[0] = advance(steps, first, start_latent)


def local(latents, start_latent, t_index, dt_units, w_time, w_in, w_up, w_down, w_out):
    zs, devices = lax.axis_size("z"), lax.axis_size("tp")
    tok_rows, channels = latents.shape[1:]
    width = w_in.shape[1]
    hid = w_up.shape[1]
    tokens = tok_rows * devices
    packed = jax.ShapeDtypeStruct((MODS_AT, LANES), F32)
    w_time_t = w_time.T
    weights = (w_in, w_out.T, w_up, w_down)

    sent, factor, *here = call(
        prepare,
        [jax.ShapeDtypeStruct((devices, 16, LANES), F32), packed]
        + [jax.ShapeDtypeStruct(w.shape, BF16) for w in weights],
        [SMEM] * 2 + [HBM] * 6,
        "prepare",
        scratch=[
            pltpu.VMEM(latents.shape, F32),
            pltpu.VMEM(w_time_t.shape, BF16),
            pltpu.SemaphoreType.DMA((6,)),
        ],
    )(t_index, dt_units, *held(latents, w_time_t, *weights))
    got = lax.all_to_all(sent, "tp", 0, 0, tiled=True)
    sent = call(
        block,
        jax.ShapeDtypeStruct((2, devices, MODS_AT, LANES), F32),
        [VMEM] * 6,
        "block",
        flops=2 * tokens * width * (hid + channels) + 2 * hid * width * channels,
        scratch=[
            pltpu.VMEM((tokens, width), F32),
            pltpu.VMEM((tokens, width), BF16),
        ],
        limit=32,
    )(got, factor, *here)
    sent = sent.reshape(2 * devices, MODS_AT, LANES)
    parts = lax.all_to_all(sent, ("core", "tp"), 0, 0, tiled=True)
    parts = parts.reshape(2, devices, MODS_AT, LANES)
    sent, first = call(
        combine,
        (jax.ShapeDtypeStruct((zs, MODS_AT, LANES), BF16), packed),
        [VMEM],
        "combine",
    )(parts)
    steps = lax.all_to_all(sent, "z", 0, 0, tiled=True)
    sent = call(
        judge,
        jax.ShapeDtypeStruct((devices, 1, LANES), F32),
        [VMEM] * 4,
        "judge",
    )(steps, first, start_latent, latents)
    totals = lax.all_to_all(sent, "tp", 0, 0, tiled=True)
    new_latents = call(
        finish,
        jax.ShapeDtypeStruct(latents.shape, F32),
        [VMEM] * 3,
        "finish",
        flops=1 << 22,
    )(steps, first, start_latent)
    step_error = jnp.sum(totals[:, 0, 0]).reshape(1)
    return (new_latents, step_error)


def solution(mesh):
    tm, tp = (mesh.shape["tm"], mesh.shape["tp"])
    grid = Mesh(mesh.devices.reshape(tm // 2, 2, tp), ("z", "core", "tp"))
    steps = ("z", "core")
    in_specs = (
        P(steps, "tp", None),
        P("tp", None),
        P(steps),
        P(steps),
        P(None, "tp"),
        P(),
        P(None, "tp"),
        P("tp", None),
        P(),
    )
    out_specs = (P(steps, "tp", None), P(steps))
    return jax.shard_map(local, mesh=grid, in_specs=in_specs, out_specs=out_specs, check_vma=False)
```

time: 81.1 us -> 73.3 us (0.904)
  local copies, waits for them, and re-layouts: 9.67 us -> 0.01 us
  blocking collectives: 47.6 us -> 52.6 us
  starting transfers between devices: 9.21 us -> 4.69 us
  waiting for transfers between devices: 2.96 us -> 5.57 us
  between operations: 3.74 us -> 1.95 us
  Pallas kernels: 6.65 us -> 7.52 us
    unnamed x22 -> x4, local copies, waits for them, and re-layouts: 9.67 us -> 0.01 us
    all_to_all x1, starting transfers between devices: 9.21 us -> 4.69 us  [local(): totals = lax.all_to_all(sent, 'tp', 0, 0, tiled=True)]
    all_to_all x1, blocking collectives: 10.6 us -> 15 us  [local(): got = lax.all_to_all(sent, 'tp', 0, 0, tiled=True)]
    all_to_all x1, waiting for transfers between devices: 2.96 us -> 5.57 us  [local(): totals = lax.all_to_all(sent, 'tp', 0, 0, tiled=True)]
    pallas_call x5, Pallas kernels: 6.65 us -> 7.52 us  [the longest x1 3.21 us: local(): call(block, jax.ShapeDtypeStruct((2, devices, MODS_AT, LANES), F32), [VME...]
where the time goes in v3:
time: 73.3 us; the launch traced here: 73 us
  blocking collectives  52.6 us (72%)
  Pallas kernels  7.52 us (10%)
  waiting for transfers between devices  5.57 us (8%)
  starting transfers between devices  4.69 us (6%)
  between operations  1.95 us (3%)
    all_to_all x1, blocking collectives, local(): steps = lax.all_to_all(sent, 'z', 0, 0, tiled=True)  26.4 us
    all_to_all x1, blocking collectives, local(): got = lax.all_to_all(sent, 'tp', 0, 0, tiled=True)  15 us
    all_to_all x1, blocking collectives, local(): parts = lax.all_to_all(sent, ('core', 'tp'), 0, 0, tiled=True)  11.2 us
    all_to_all x1, waiting for transfers between devices, local(): totals = lax.all_to_all(sent, 'tp', 0, 0, tiled=True)  5.57 us
    all_to_all x1, starting transfers between devices, local(): totals = lax.all_to_all(sent, 'tp', 0, 0, tiled=True)  4.69 us
    pallas_call x1, Pallas kernels, local(): call(block, jax.ShapeDtypeStruct((2, devices, MODS_AT, LANES), F32), [VME...  3.21 us
    pallas_call x1, Pallas kernels, local(): call(prepare, [jax.ShapeDtypeStruct((devices, 16, LANES), F32), packed] +...  2.79 us
  transfers between devices with their start and end apart: 1, of which 1 were waited for; matrix products, arithmetic and copies ran while one was open for 0% of the time, Pallas kernels for 1%

profile of v3, /device:TPU:2, one launch (start us, length us, event | category | flops | bytes accessed | tf_op | source)
XLA Modules:
  0.0 73.0 jit_solution(5672635364483620971)
XLA Ops:
  1.9 2.8 %prepare.1 = (f32[16,16,128]{2,1,0:T(8,128)S(1)}, f32[8,128]{1,0:T(8,128)S(1)}, bf16[64,3072]{1,0:T(8,128)(2,1)S(1)}, bf16[64,3072]{1,0:T(8,128)(2,1)S(1)}, bf16...) custom-call(s32[1]{0:T(128)S(6)} %copy.11.t_index, s32[1]{0:T(128)S(6)} %copy.12.dt_units, f32[1,16,64]{2,1,0:T(8,128)} %latents.3, ...), custom_call_target="tpu_custom_call" | custom-call | bytes 1048576 | tf_op jit(solution)/shard_map/prepare/pallas_call | solution.py:190
  4.7 15.0 %all_to_all.20.got = f32[16,16,128]{2,1,0:T(8,128)S(1)} all-to-all(f32[16,16,128]{2,1,0:T(8,128)S(1)} %get-tuple-element.10), channel_id=1, replica_groups=mesh['z'=16,'core'=2,'tp'=16] {'tp'}, dimensions={0} | all-to-all | bytes 262144 | tf_op jit(solution)/shard_map/all_to_all | solution.py:202
  19.8 0.0 copy-start
  19.8 0.0 copy-start.1
  19.8 3.2 %block.1 = f32[2,16,8,128]{3,2,1,0:T(8,128)S(1)} custom-call(f32[16,16,128]{2,1,0:T(8,128)S(1)} %all_to_all.20.got, f32[8,128]{1,0:T(8,128)S(1)} %get-tuple-element.11.factor, bf16[64,3072]{1,0:T(8,128)(2,1)S(1)} %get-tuple-element.12.w_in, bf16[64,3072]{1,0:T(8,128)(2,1)S(1)} %get-tuple-element.13.w_out_t, bf16[3072,384]{1,0:T(8,128)(2,1)S(1)} %get-tuple-element.14.w_up, ...), custom_call_target="tpu_custom_call" | custom-call | flops 855638016 | bytes 1048576 | tf_op jit(solution)/shard_map/block/pallas_call | solution.py:203
  23.0 11.2 %all_to_all.21 = f32[32,8,128]{2,1,0:T(8,128)S(1)} all-to-all(f32[32,8,128]{2,1,0:T(8,128)S(1)} %bitcast.5), channel_id=1, replica_groups=mesh['z'=16,'core'=2,'tp'=16] {'core','tp'}, dimensions={0} | all-to-all | bytes 262144 | tf_op jit(solution)/shard_map/all_to_all | solution.py:216
  34.2 26.4 %all_to_all.22.steps = bf16[16,8,128]{2,1,0:T(8,128)(2,1)S(1)} all-to-all(bf16[16,8,128]{2,1,0:T(8,128)(2,1)S(1)} %get-tuple-element.16), channel_id=1, replica_groups=mesh['z'=16,'core'=2,'tp'=16] {'z'}, dimensions={0} | all-to-all | bytes 65536 | tf_op jit(solution)/shard_map/all_to_all | solution.py:224
  60.6 0.0 copy-done
  60.6 0.0 copy-done.1
  60.6 0.8 %judge.1 = f32[16,1,128]{2,1,0:T(1,128)} custom-call(bf16[16,8,128]{2,1,0:T(8,128)(2,1)S(1)} %all_to_all.22.steps, f32[8,128]{1,0:T(8,128)S(1)} %get-tuple-element.17.first, f32[16,64]{1,0:T(8,128)S(1)} %copy-done.1, f32[1,16,64]{2,1,0:T(8,128)S(1)} %copy-done), custom_call_target="tpu_custom_call" | custom-call | bytes 1048576 | tf_op jit(solution)/shard_map/judge/pallas_call | solution.py:225
  61.4 4.7 %all-to-all-start.3 = ((f32[16,1,128]{2,1,0:T(1,128)}), f32[16,1,128]{2,1,0:T(1,128)S(1)}, u32[]{:S(2)}, u32[]{:S(2)}) async-start(f32[16,1,128]{2,1,0:T(1,128)} %judge.1), calls=%async_computation.3 | async-start | bytes 16384 | tf_op jit(solution)/shard_map/all_to_all | solution.py:231
  66.1 0.7 finish.1
  66.8 5.6 %all-to-all-done.3 = f32[16,1,128]{2,1,0:T(1,128)S(1)} async-done(((f32[16,1,128]{2,1,0:T(1,128)}), f32[16,1,128]{2,1,0:T(1,128)S(1)}, u32[]{:S(2)}, u32[]{:S(2)}) %all-to-all-start.3) | async-done | bytes 8224 | tf_op jit(solution)/shard_map/all_to_all | solution.py:231
  72.4 0.6 slice_reduce_fusion
  (1 shorter events, 0.0 us)
Async XLA Ops:
  19.8 40.9 %copy-start = (f32[1,16,64]{2,1,0:T(8,128)S(1)}, f32[1,16,64]{2,1,0:T(8,128)}, u32[]{:S(2)}) copy-start(f32[1,16,64]{2,1,0:T(8,128)} %latents.3) | copy-start | bytes 12292
  19.8 40.9 %copy-start.1 = (f32[16,64]{1,0:T(8,128)S(1)}, f32[16,64]{1,0:T(8,128)}, u32[]{:S(2)}) copy-start(f32[16,64]{1,0:T(8,128)} %start_latent.3) | copy-start | bytes 12292
  61.4 10.9 %all-to-all-start.3 = ((f32[16,1,128]{2,1,0:T(1,128)}), f32[16,1,128]{2,1,0:T(1,128)S(1)}, u32[]{:S(2)}, u32[]{:S(2)}) async-start(f32[16,1,128]{2,1,0:T(1,128)} %judge.1), calls=%async_computation.3 | async-start | bytes 16384 | tf_op jit(solution)/shard_map/all_to_all | solution.py:231

commit v4 on v3

--- a/solution.py
+++ b/solution.py
@@ -1,3 +1,5 @@
+import math
+
 import jax
 import jax.numpy as jnp
 from jax import lax
@@ -8,6 +10,9 @@
 
 LANES = 128
 MODS_AT = 8
+NEAR = 4
+AXES = ("far", "near", "core", "y", "x")
+TP = AXES[3:]
 SMEM = pl.BlockSpec(memory_space=pltpu.SMEM)
 VMEM = pl.BlockSpec(memory_space=pltpu.VMEM)
 HBM = pl.BlockSpec(memory_space=pltpu.HBM)
@@ -57,7 +62,7 @@
     return high, value - high
 
 
-def prepare(t_index, dt_units, latents, w_time, *refs):
+def prepare(t_index, dt_units, flag, latents, w_time, *refs):
     weights, (sent, factor), here = refs[:4], refs[4:6], refs[6:10]
     lat_here, w_here, sems = refs[10:]
     pairs = [(w_time, w_here), (latents, lat_here)]
@@ -74,7 +79,7 @@
     dims = (((1,), (1,)), ((), ()))
     mods = lax.dot_general(emb, w_here[...], dims, preferred_element_type=F32)[:1]
     gap = jnp.zeros((1, LANES // 2), F32)
-    odd = lax.axis_index("tp") % 2 == 1
+    odd = lax.axis_index(TP) % 2 == 1
     mods = jnp.where(odd, jnp.concatenate([gap, mods], 1), jnp.concatenate([mods, gap], 1))
     lines = mods.shape[1] // LANES
     rows = [lat] + [mods[:, i * LANES : (i + 1) * LANES] for i in range(lines)]
@@ -115,7 +120,7 @@
         hidden[:, start : start + step] = part
         for at in range(0, step, LANES):
             total = total + part[:, at : at + LANES]
-    place = pl.multiple_of(lax.axis_index("tp") * MODS_AT, MODS_AT)
+    place = pl.multiple_of(lax.axis_index(TP) * MODS_AT, MODS_AT)
     own = [hidden[pl.ds(place + at, MODS_AT), :] for at in (0, tokens // 2)]
     high, low = split(jnp.concatenate(own, axis=0))
     rest, last = split(low)
@@ -140,13 +145,13 @@
     half = tokens // 2
     part = jnp.where(left((half, LANES)), part[:half], part[half:])
     part = part.reshape(devices, MODS_AT, LANES)
-    mine = lax.broadcasted_iota(jnp.int32, part.shape, 0) == lax.axis_index("tp")
+    mine = lax.broadcasted_iota(jnp.int32, part.shape, 0) == lax.axis_index(TP)
     part = jnp.where(mine, part + own[None], part) * factor[...][None]
     sent[0] = part
     sent[1] = part
 
 
-def combine(parts, sent, first):
+def combine(parts, sent, near, first):
     one = parts[0, 0]
     two = parts[1, 0]
     for device in range(1, parts.shape[1]):
@@ -156,12 +161,15 @@
     both = (one + two).astype(BF16)
     for device in range(sent.shape[0]):
         sent[device] = both
+    for device in range(near.shape[0]):
+        near[device] = both
 
 
 def advance(steps, first, start_latent):
     before = jnp.where(lax.axis_index("core") == 1, first[...], 0.0)
+    here = lax.axis_index(AXES[:2])
     for z in range(steps.shape[0]):
-        before = before + jnp.where(z < lax.axis_index("z"), steps[z].astype(F32), 0.0)
+        before = before + jnp.where(z < here, steps[z].astype(F32), 0.0)
     half = LANES // 2
     before = jnp.concatenate([before[:, :half], before[:, half:]], axis=0)
     return start_latent[...] + before
@@ -169,7 +177,7 @@
 
 def judge(steps, first, start_latent, latents, sent):
     change = advance(steps, first, start_latent) - latents[0]
-    count = change.size * sent.shape[0]
+    count = change.size * lax.axis_size(TP)
     sent[...] = jnp.full(sent.shape, jnp.sum(change * change) / count, F32)
 
 
@@ -178,7 +186,7 @@
 
 
 def local(latents, start_latent, t_index, dt_units, w_time, w_in, w_up, w_down, w_out):
-    zs, devices = lax.axis_size("z"), lax.axis_size("tp")
+    zs, devices = lax.axis_size(AXES[:2]), lax.axis_size(TP)
     tok_rows, channels = latents.shape[1:]
     width = w_in.shape[1]
     hid = w_up.shape[1]
@@ -187,19 +195,20 @@
     w_time_t = w_time.T
     weights = (w_in, w_out.T, w_up, w_down)
 
+    early = lax.axis_index("far") == 0
     sent, factor, *here = call(
         prepare,
         [jax.ShapeDtypeStruct((devices, 16, LANES), F32), packed]
         + [jax.ShapeDtypeStruct(w.shape, BF16) for w in weights],
-        [SMEM] * 2 + [HBM] * 6,
+        [SMEM] * 3 + [HBM] * 6,
         "prepare",
         scratch=[
             pltpu.VMEM(latents.shape, F32),
             pltpu.VMEM(w_time_t.shape, BF16),
             pltpu.SemaphoreType.DMA((6,)),
         ],
-    )(t_index, dt_units, *held(latents, w_time_t, *weights))
-    got = lax.all_to_all(sent, "tp", 0, 0, tiled=True)
+    )(t_index, dt_units, early.astype(jnp.int32).reshape(1), *held(latents, w_time_t, *weights))
+    got = lax.all_to_all(sent, TP, 0, 0, tiled=True)
     sent = call(
         block,
         jax.ShapeDtypeStruct((2, devices, MODS_AT, LANES), F32),
@@ -213,22 +222,40 @@
         limit=32,
     )(got, factor, *here)
     sent = sent.reshape(2 * devices, MODS_AT, LANES)
-    parts = lax.all_to_all(sent, ("core", "tp"), 0, 0, tiled=True)
+    parts = lax.all_to_all(sent, AXES[2:], 0, 0, tiled=True)
     parts = parts.reshape(2, devices, MODS_AT, LANES)
-    sent, first = call(
+    sent, close, first = call(
         combine,
-        (jax.ShapeDtypeStruct((zs, MODS_AT, LANES), BF16), packed),
+        [jax.ShapeDtypeStruct((n, MODS_AT, LANES), BF16) for n in (zs, NEAR)] + [packed],
         [VMEM],
         "combine",
     )(parts)
-    steps = lax.all_to_all(sent, "z", 0, 0, tiled=True)
-    sent = call(
-        judge,
-        jax.ShapeDtypeStruct((devices, 1, LANES), F32),
-        [VMEM] * 4,
-        "judge",
-    )(steps, first, start_latent, latents)
-    totals = lax.all_to_all(sent, "tp", 0, 0, tiled=True)
+
+    def errors(steps, *shape):
+        return call(
+            judge,
+            jax.ShapeDtypeStruct(shape + (LANES,), F32),
+            [VMEM] * 4,
+            "judge",
+        )(steps, first, start_latent, latents)
+
+    def ahead(close):
+        return errors(lax.all_to_all(close, "near", 0, 0, tiled=True), MODS_AT)
+
+    def gather(part):
+        part = part[:1]
+        for axis in ("x", "y"):
+            part = jnp.sum(lax.all_gather(part, axis), axis=0)
+        return part[0, :1]
+
+    def exchange(steps):
+        totals = lax.all_to_all(errors(steps, devices, 1), TP, 0, 0, tiled=True)
+        return jnp.sum(totals[:, 0, 0]).reshape(1)
+
+    part = lax.cond(early, ahead, lambda close: first, close)
+    steps = lax.all_to_all(sent, AXES[:2], 0, 0, tiled=True)
+    soon = lax.cond(early, gather, lambda part: part[0, :1], part)
+    step_error = lax.cond(early, lambda steps: soon, exchange, steps)
     new_latents = call(
         finish,
         jax.ShapeDtypeStruct(latents.shape, F32),
@@ -236,24 +263,24 @@
         "finish",
         flops=1 << 22,
     )(steps, first, start_latent)
-    step_error = jnp.sum(totals[:, 0, 0]).reshape(1)
     return (new_latents, step_error)
 
 
 def solution(mesh):
     tm, tp = (mesh.shape["tm"], mesh.shape["tp"])
-    grid = Mesh(mesh.devices.reshape(tm // 2, 2, tp), ("z", "core", "tp"))
-    steps = ("z", "core")
+    side = math.isqrt(tp)
+    grid = Mesh(mesh.devices.reshape(tm // 2 // NEAR, NEAR, 2, side, side), AXES)
+    steps = AXES[:3]
     in_specs = (
-        P(steps, "tp", None),
-        P("tp", None),
+        P(steps, TP, None),
+        P(TP, None),
         P(steps),
         P(steps),
-        P(None, "tp"),
+        P(None, TP),
         P(),
-        P(None, "tp"),
-        P("tp", None),
+        P(None, TP),
+        P(TP, None),
         P(),
     )
-    out_specs = (P(steps, "tp", None), P(steps))
+    out_specs = (P(steps, TP, None), P(steps))
     return jax.shard_map(local, mesh=grid, in_specs=in_specs, out_specs=out_specs, check_vma=False)

time: 73.3 us -> 68.7 us (0.937)
  the two profiles are of different devices: /device:TPU:2 before, /device:TPU:128 now
where the time goes in v4:
time: 68.7 us; the launch traced here: 68.4 us
  blocking collectives  36.7 us (53%)
  starting transfers between devices  13.9 us (20%)
  Pallas kernels  7.53 us (11%)
  waiting for transfers between devices  7.27 us (11%)
  between operations  1.95 us (3%)
    all_to_all x1, blocking collectives, local(): got = lax.all_to_all(sent, TP, 0, 0, tiled=True)  14.8 us
    all_to_all x1, starting transfers between devices, local(): steps = lax.all_to_all(sent, AXES[:2], 0, 0, tiled=True)  13.9 us
    all_to_all x1, blocking collectives, local(): parts = lax.all_to_all(sent, AXES[2:], 0, 0, tiled=True)  11.2 us
    all_to_all x1, blocking collectives, exchange(): totals = lax.all_to_all(errors(steps, devices, 1), TP, 0, 0, tiled=True)  10.7 us
    all_to_all x1, waiting for transfers between devices, local(): steps = lax.all_to_all(sent, AXES[:2], 0, 0, tiled=True)  7.27 us
    pallas_call x1, Pallas kernels, local(): call(block, jax.ShapeDtypeStruct((2, devices, MODS_AT, LANES), F32), [VME...  3.21 us
    pallas_call x1, Pallas kernels, local(): call(prepare, [jax.ShapeDtypeStruct((devices, 16, LANES), F32), packed] +...  2.8 us
  transfers between devices with their start and end apart: 1, of which 1 were waited for; matrix products, arithmetic and copies ran while one was open for 1% of the time, Pallas kernels for 0%

profile of v4, /device:TPU:128, one launch (start us, length us, event | category | flops | bytes accessed | tf_op | source)
XLA Modules:
  0.0 68.4 jit_solution(8723144257814059478)
XLA Ops:
  1.9 2.8 %prepare.1 = (f32[16,16,128]{2,1,0:T(8,128)S(1)}, f32[8,128]{1,0:T(8,128)S(1)}, bf16[64,3072]{1,0:T(8,128)(2,1)S(1)}, bf16[64,3072]{1,0:T(8,128)(2,1)S(1)}, bf16...) custom-call(s32[1]{0:T(128)S(6)} %copy.17.t_index, s32[1]{0:T(128)S(6)} %copy.18.dt_units, s32[1]{0:T(128)} %bitcast.6.flag, ...), custom_call_target="tpu_custom_call" | custom-call | bytes 1048576 | tf_op jit(solution)/shard_map/prepare/pallas_call | solution.py:199
  4.7 14.8 %all_to_all.25.got = f32[16,16,128]{2,1,0:T(8,128)S(1)} all-to-all(f32[16,16,128]{2,1,0:T(8,128)S(1)} %get-tuple-element.48), channel_id=1, replica_groups=mesh['far'=4,'near'=4,'core'=2,'y'=4,'x'=4] {'y','x'}, dimensions={0} | all-to-all | bytes 262144 | tf_op jit(solution)/shard_map/all_to_all | solution.py:211
  19.6 0.0 copy-start
  19.6 0.0 copy-start.1
  19.6 3.2 %block.1 = f32[2,16,8,128]{3,2,1,0:T(8,128)S(1)} custom-call(f32[16,16,128]{2,1,0:T(8,128)S(1)} %all_to_all.25.got, f32[8,128]{1,0:T(8,128)S(1)} %get-tuple-element.49.factor, bf16[64,3072]{1,0:T(8,128)(2,1)S(1)} %get-tuple-element.50.w_in, bf16[64,3072]{1,0:T(8,128)(2,1)S(1)} %get-tuple-element.51.w_out_t, bf16[3072,384]{1,0:T(8,128)(2,1)S(1)} %get-tuple-element.52.w_up, ...), custom_call_target="tpu_custom_call" | custom-call | flops 855638016 | bytes 1048576 | tf_op jit(solution)/shard_map/block/pallas_call | solution.py:212
  22.8 11.2 %all_to_all.26 = f32[32,8,128]{2,1,0:T(8,128)S(1)} all-to-all(f32[32,8,128]{2,1,0:T(8,128)S(1)} %bitcast.13), channel_id=1, replica_groups=mesh['far'=4,'near'=4,'core'=2,'y'=4,'x'=4] {'core','y','x'}, dimensions={0} | all-to-all | bytes 262144 | tf_op jit(solution)/shard_map/all_to_all | solution.py:225
  34.0 0.6 combine.1
  34.6 0.0 copy-done
  34.6 0.0 copy-done.1
  34.6 13.9 %all-to-all-start.4 = ((bf16[16,8,128]{2,1,0:T(8,128)(2,1)}), bf16[16,8,128]{2,1,0:T(8,128)(2,1)S(1)}, u32[]{:S(2)}, u32[]{:S(2)}) async-start(bf16[16,8,128]{2,1,0:T(8,128)(2,1)} %get-tuple-element.54), calls=%async_computation.4 | async-start | bytes 65536 | tf_op jit(solution)/shard_map/all_to_all | solution.py:256
  48.5 0.5 conditional.4
  48.5 0.5 slice.8
  49.0 7.3 %all-to-all-done.4.steps = bf16[16,8,128]{2,1,0:T(8,128)(2,1)S(1)} async-done(((bf16[16,8,128]{2,1,0:T(8,128)(2,1)}), bf16[16,8,128]{2,1,0:T(8,128)(2,1)S(1)}, u32[]{:S(2)}, u32[]{:S(2)}) %all-to-all-start.4) | async-done | bytes 32800 | tf_op jit(solution)/shard_map/all_to_all | solution.py:256
  56.2 11.5 %conditional.5 = (f32[1]{0:T(128)}) conditional(s32[]{:T(128)} %convert_element_type.2, (bf16[16,8,128]{2,1,0:T(8,128)(2,1)S(1)}, f32[8,128]{1,0:T(8,128)S(1)}, f32[16,64]{1,0:T(8,128)S(1)}, f32[1,16,64]{2,1,0:T(8,128)S(1)}) %tuple.38, f32[1]{0:T(128)} %get-tuple-element.58), branch_computations={%region_6.0_spmd, %region_8.0_spmd} | conditional | flops 15 | bytes 1065036 | solution.py:258
  56.2 0.2 judge.3
  56.5 10.7 %all_to_all.24 = f32[16,1,128]{2,1,0:T(1,128)S(1)} all-to-all(f32[16,1,128]{2,1,0:T(1,128)S(1)} %judge.3), channel_id=1, replica_groups=mesh['far'=4,'near'=4,'core'=2,'y'=4,'x'=4] {'y','x'}, dimensions={0} | all-to-all | bytes 16384 | tf_op jit(solution)/shard_map/cond/branch_0_fun/all_to_all | solution.py:252
  67.1 0.6 slice_reduce_fusion
  67.7 0.7 %finish.1 = f32[1,16,64]{2,1,0:T(8,128)} custom-call(bf16[16,8,128]{2,1,0:T(8,128)(2,1)S(1)} %all-to-all-done.4.steps, f32[8,128]{1,0:T(8,128)S(1)} %get-tuple-element.55.first, f32[16,64]{1,0:T(8,128)S(1)} %copy-done.1), custom_call_target="tpu_custom_call" | custom-call | flops 4194304 | bytes 1048576 | tf_op jit(solution)/shard_map/finish/pallas_call | solution.py:259
  (2 shorter events, 0.0 us)
Async XLA Ops:
  19.6 15.0 %copy-start = (f32[1,16,64]{2,1,0:T(8,128)S(1)}, f32[1,16,64]{2,1,0:T(8,128)}, u32[]{:S(2)}) copy-start(f32[1,16,64]{2,1,0:T(8,128)} %latents.1) | copy-start | bytes 12292
  19.6 15.0 %copy-start.1 = (f32[16,64]{1,0:T(8,128)S(1)}, f32[16,64]{1,0:T(8,128)}, u32[]{:S(2)}) copy-start(f32[16,64]{1,0:T(8,128)} %start_latent.1) | copy-start | bytes 12292
  34.6 21.6 %all-to-all-start.4 = ((bf16[16,8,128]{2,1,0:T(8,128)(2,1)}), bf16[16,8,128]{2,1,0:T(8,128)(2,1)S(1)}, u32[]{:S(2)}, u32[]{:S(2)}) async-start(bf16[16,8,128]{2,1,0:T(8,128)(2,1)} %get-tuple-element.54), calls=%async_computation.4 | async-start | bytes 65536 | tf_op jit(solution)/shard_map/all_to_all | solution.py:256

commit v5 on v4

--- a/solution.py
+++ b/solution.py
@@ -20,12 +20,12 @@
 BF16 = jnp.bfloat16
 
 
-def call(body, out_shape, in_specs, name, flops=0, scratch=(), limit=16):
+def call(body, out_shape, in_specs, name, flops=0, scratch=(), limit=16, out_specs=None):
     return pl.pallas_call(
         body,
         out_shape=out_shape,
         in_specs=in_specs,
-        out_specs=jax.tree.map(lambda _: VMEM, out_shape),
+        out_specs=out_specs or jax.tree.map(lambda _: VMEM, out_shape),
         scratch_shapes=list(scratch),
         cost_estimate=pl.CostEstimate(flops=flops, bytes_accessed=1 << 20, transcendentals=0),
         compiler_params=pltpu.CompilerParams(vmem_limit_bytes=limit << 20),
@@ -63,10 +63,8 @@
 
 
 def prepare(t_index, dt_units, flag, latents, w_time, *refs):
-    weights, (sent, factor), here = refs[:4], refs[4:6], refs[6:10]
-    lat_here, w_here, sems = refs[10:]
-    pairs = [(w_time, w_here), (latents, lat_here)]
-    copies = load(pairs + list(zip(weights, here)), sems)
+    sent, factor, lat_here, w_here, sems = refs
+    copies = load([(w_time, w_here), (latents, lat_here)], sems)
     half = w_here.shape[1] // 2
     order = lax.broadcasted_iota(jnp.int32, (16, half), 1).astype(F32)
     freqs = jnp.exp(-jnp.log(jnp.full((16, half), 10000.0, F32)) * order / half)
@@ -87,8 +85,6 @@
     block = jnp.concatenate(rows, axis=0)
     for device in range(sent.shape[0]):
         sent[device] = block
-    for copy in copies[2:]:
-        copy.wait()
 
 
 def block(got, factor, w_in, w_out_t, w_up, w_down, sent, hidden, normed):
@@ -181,8 +177,9 @@
     sent[...] = jnp.full(sent.shape, jnp.sum(change * change) / count, F32)
 
 
-def finish(steps, first, start_latent, new_latents):
+def finish(parts, steps, first, start_latent, new_latents, step_error):
     new_latents[0] = advance(steps, first, start_latent)
+    step_error[0] = jnp.sum(parts[...], axis=0)[0, 0]
 
 
 def local(latents, start_latent, t_index, dt_units, w_time, w_in, w_up, w_down, w_out):
@@ -196,18 +193,18 @@
     weights = (w_in, w_out.T, w_up, w_down)
 
     early = lax.axis_index("far") == 0
-    sent, factor, *here = call(
+    sent, factor = call(
         prepare,
-        [jax.ShapeDtypeStruct((devices, 16, LANES), F32), packed]
-        + [jax.ShapeDtypeStruct(w.shape, BF16) for w in weights],
-        [SMEM] * 3 + [HBM] * 6,
+        [jax.ShapeDtypeStruct((devices, 16, LANES), F32), packed],
+        [SMEM] * 3 + [HBM] * 2,
         "prepare",
+        flops=1 << 34,
         scratch=[
             pltpu.VMEM(latents.shape, F32),
             pltpu.VMEM(w_time_t.shape, BF16),
-            pltpu.SemaphoreType.DMA((6,)),
+            pltpu.SemaphoreType.DMA((2,)),
         ],
-    )(t_index, dt_units, early.astype(jnp.int32).reshape(1), *held(latents, w_time_t, *weights))
+    )(t_index, dt_units, early.astype(jnp.int32).reshape(1), *held(latents, w_time_t))
     got = lax.all_to_all(sent, TP, 0, 0, tiled=True)
     sent = call(
         block,
@@ -220,7 +217,7 @@
             pltpu.VMEM((tokens, width), BF16),
         ],
         limit=32,
-    )(got, factor, *here)
+    )(got, factor, *weights)
     sent = sent.reshape(2 * devices, MODS_AT, LANES)
     parts = lax.all_to_all(sent, AXES[2:], 0, 0, tiled=True)
     parts = parts.reshape(2, devices, MODS_AT, LANES)
@@ -243,26 +240,26 @@
         return errors(lax.all_to_all(close, "near", 0, 0, tiled=True), MODS_AT)
 
     def gather(part):
-        part = part[:1]
-        for axis in ("x", "y"):
-            part = jnp.sum(lax.all_gather(part, axis), axis=0)
-        return part[0, :1]
-
-    def exchange(steps):
+        part = jnp.sum(lax.all_gather(part[:1], "x"), axis=0)
+        return lax.all_gather(part, "y")
+
+    def close_up(parts, steps):
+        return call(
+            finish,
+            (jax.ShapeDtypeStruct(latents.shape, F32), jax.ShapeDtypeStruct((1,), F32)),
+            [VMEM] * 4,
+            "finish",
+            out_specs=(VMEM, SMEM),
+        )(parts, steps, first, start_latent)
+
+    def exchange(parts, steps):
         totals = lax.all_to_all(errors(steps, devices, 1), TP, 0, 0, tiled=True)
-        return jnp.sum(totals[:, 0, 0]).reshape(1)
+        return close_up(totals, steps)
 
     part = lax.cond(early, ahead, lambda close: first, close)
     steps = lax.all_to_all(sent, AXES[:2], 0, 0, tiled=True)
-    soon = lax.cond(early, gather, lambda part: part[0, :1], part)
-    step_error = lax.cond(early, lambda steps: soon, exchange, steps)
-    new_latents = call(
-        finish,
-        jax.ShapeDtypeStruct(latents.shape, F32),
-        [VMEM] * 3,
-        "finish",
-        flops=1 << 22,
-    )(steps, first, start_latent)
+    soon = lax.cond(early, gather, lambda part: part[: lax.axis_size("y"), None], part)
+    new_latents, step_error = lax.cond(early, close_up, exchange, soon, steps)
     return (new_latents, step_error)
 
 

time: 68.7 us -> 67 us (0.975)
  Pallas kernels: 7.53 us -> 6.16 us
    pallas_call x2, Pallas kernels: 3.48 us -> 2.11 us  [the longest x1 1.4 us: local(): call(prepare, [jax.ShapeDtypeStruct((devices, 16, LANES), F32), packed],...]
  transfers between devices with their start and end apart: 1 -> 1, of which waited for: 1 -> 1; matrix products, arithmetic and copies ran while one was open for 1% -> 0% of each run, Pallas kernels for 0% -> 0%
where the time goes in v5:
time: 67 us; the launch traced here: 66.7 us
  blocking collectives  36.8 us (55%)
  starting transfers between devices  13.9 us (21%)
  waiting for transfers between devices  7.76 us (12%)
  Pallas kernels  6.16 us (9%)
  between operations  2.02 us (3%)
    all_to_all x1, blocking collectives, local(): got = lax.all_to_all(sent, TP, 0, 0, tiled=True)  15 us
    all_to_all x1, starting transfers between devices, local(): steps = lax.all_to_all(sent, AXES[:2], 0, 0, tiled=True)  13.9 us
    all_to_all x1, blocking collectives, local(): parts = lax.all_to_all(sent, AXES[2:], 0, 0, tiled=True)  11.2 us
    all_to_all x1, blocking collectives, exchange(): totals = lax.all_to_all(errors(steps, devices, 1), TP, 0, 0, tiled=True)  10.7 us
    all_to_all x1, waiting for transfers between devices, local(): steps = lax.all_to_all(sent, AXES[:2], 0, 0, tiled=True)  7.76 us
    pallas_call x1, Pallas kernels, local(): call(block, jax.ShapeDtypeStruct((2, devices, MODS_AT, LANES), F32), [VME...  3.21 us
    pallas_call x1, Pallas kernels, local(): call(prepare, [jax.ShapeDtypeStruct((devices, 16, LANES), F32), packed],...  1.4 us
  transfers between devices with their start and end apart: 1, of which 1 were waited for; matrix products, arithmetic and copies ran while one was open for 0% of the time, Pallas kernels for 0%

profile of v5, /device:TPU:128, one launch (start us, length us, event | category | flops | bytes accessed | tf_op | source)
XLA Modules:
  0.0 66.7 jit_solution(12886040034640513589)
XLA Ops:
  1.9 0.0 copy-start
  1.9 0.0 copy-start.1
  1.9 0.0 copy-start.2
  2.0 0.0 copy-start.3
  2.0 1.4 %prepare.1 = (f32[16,16,128]{2,1,0:T(8,128)S(1)}, f32[8,128]{1,0:T(8,128)S(1)}) custom-call(s32[1]{0:T(128)S(6)} %copy.23.t_index, s32[1]{0:T(128)S(6)} %copy.24.dt_units, s32[1]{0:T(128)} %bitcast.3.flag, f32[1,16,64]{2,1,0:T(8,128)} %latents.1, bf16[576,256]{1,0:T(8,128)(2,1)} %bitcast.14), custom_call_target="tpu_custom_call" | custom-call | flops 17179869184 | bytes 1048576 | tf_op jit(solution)/shard_map/prepare/pallas_call | solution.py:196
  3.4 15.0 %all_to_all.25.got = f32[16,16,128]{2,1,0:T(8,128)S(1)} all-to-all(f32[16,16,128]{2,1,0:T(8,128)S(1)} %get-tuple-element.52), channel_id=1, replica_groups=mesh['far'=4,'near'=4,'core'=2,'y'=4,'x'=4] {'y','x'}, dimensions={0} | all-to-all | bytes 262144 | tf_op jit(solution)/shard_map/all_to_all | solution.py:208
  18.3 0.0 copy-done
  18.3 0.0 copy-done.1
  18.3 0.0 copy-done.2
  18.3 0.0 copy-done.3
  18.4 0.0 copy-start.4
  18.4 0.0 copy-start.5
  18.4 3.2 %block.1 = f32[2,16,8,128]{3,2,1,0:T(8,128)S(1)} custom-call(f32[16,16,128]{2,1,0:T(8,128)S(1)} %all_to_all.25.got, f32[8,128]{1,0:T(8,128)S(1)} %get-tuple-element.53.factor, bf16[64,3072]{1,0:T(8,128)(2,1)S(1)} %copy-done.2, bf16[64,3072]{1,0:T(8,128)(2,1)S(1)} %bitcast.11, bf16[3072,384]{1,0:T(8,128)(2,1)S(1)} %copy-done, bf16[384,3072]{1,0:T(8,128)(2,1)S(1)} %copy-done.1), custom_call_target="tpu_custom_call" | custom-call | flops 855638016 | bytes 1048576 | tf_op jit(solution)/shard_map/block/pallas_call | solution.py:209
  21.6 11.2 %all_to_all.26 = f32[32,8,128]{2,1,0:T(8,128)S(1)} all-to-all(f32[32,8,128]{2,1,0:T(8,128)S(1)} %bitcast.9), channel_id=1, replica_groups=mesh['far'=4,'near'=4,'core'=2,'y'=4,'x'=4] {'core','y','x'}, dimensions={0} | all-to-all | bytes 262144 | tf_op jit(solution)/shard_map/all_to_all | solution.py:222
  32.8 0.6 combine.1
  33.4 0.0 copy-done.4
  33.4 0.0 copy-done.5
  33.4 13.9 %all-to-all-start.4 = ((bf16[16,8,128]{2,1,0:T(8,128)(2,1)}), bf16[16,8,128]{2,1,0:T(8,128)(2,1)S(1)}, u32[]{:S(2)}, u32[]{:S(2)}) async-start(bf16[16,8,128]{2,1,0:T(8,128)(2,1)} %get-tuple-element.54), calls=%async_computation.4 | async-start | bytes 65536 | tf_op jit(solution)/shard_map/all_to_all | solution.py:260
  47.3 7.8 %all-to-all-done.4 = bf16[16,8,128]{2,1,0:T(8,128)(2,1)S(1)} async-done(((bf16[16,8,128]{2,1,0:T(8,128)(2,1)}), bf16[16,8,128]{2,1,0:T(8,128)(2,1)S(1)}, u32[]{:S(2)}, u32[]{:S(2)}) %all-to-all-start.4) | async-done | bytes 32800 | tf_op jit(solution)/shard_map/all_to_all | solution.py:260
  55.1 11.6 %conditional.5 = ((f32[1,16,64]{2,1,0:T(8,128)}, f32[1]{0:T(128)})) conditional(s32[]{:T(128)} %convert_element_type.2, (bf16[16,8,128]{2,1,0:T(8,128)(2,1)S(1)}, f32[8,128]{1,0:T(8,128)S(1)}, f32[16,64]{1,0:T(8,128)S(1)}, f32[1,16,64]{2,1,0:T(8,128)S(1)}) %tuple.44, (f32[4,1,128]{2,1,0:T(1,128)S(1)}, bf16[16,8,128]{2,1,0:T(8,128)(2,1)S(1)}, ...), branch_computations={%region_5.0_spmd, %region_6.0_spmd} | conditional | bytes 2113544 | solution.py:262
  55.1 0.2 judge.3
  55.3 10.7 %all_to_all.24.parts = f32[16,1,128]{2,1,0:T(1,128)S(1)} all-to-all(f32[16,1,128]{2,1,0:T(1,128)S(1)} %judge.3), channel_id=1, replica_groups=mesh['far'=4,'near'=4,'core'=2,'y'=4,'x'=4] {'y','x'}, dimensions={0} | all-to-all | bytes 16384 | tf_op jit(solution)/shard_map/cond/branch_0_fun/all_to_all | solution.py:256
  65.9 0.7 %finish.2 = (f32[1,16,64]{2,1,0:T(8,128)}, f32[1]{0:T(128)}) custom-call(f32[16,1,128]{2,1,0:T(1,128)S(1)} %all_to_all.24.parts, bf16[16,8,128]{2,1,0:T(8,128)(2,1)S(1)} %get-tuple-element.37.steps, f32[8,128]{1,0:T(8,128)S(1)} %get-tuple-element.38.first, f32[16,64]{1,0:T(8,128)S(1)} %get-tuple-element.39.start_latent), custom_call_target="tpu_custom_call" | custom-call | bytes 1048576 | tf_op jit(solution)/shard_map/cond/branch_0_fun/finish/pallas_call | solution.py:247
  (4 shorter events, 0.0 us)
Async XLA Ops:
  1.9 16.4 %copy-start = (bf16[3072,384]{1,0:T(8,128)(2,1)S(1)}, bf16[3072,384]{1,0:T(8,128)(2,1)}, u32[]{:S(2)}) copy-start(bf16[3072,384]{1,0:T(8,128)(2,1)} %w_up.1) | copy-start | bytes 7077892
  1.9 16.4 %copy-start.1 = (bf16[384,3072]{1,0:T(8,128)(2,1)S(1)}, bf16[384,3072]{1,0:T(8,128)(2,1)}, u32[]{:S(2)}) copy-start(bf16[384,3072]{1,0:T(8,128)(2,1)} %w_down.1) | copy-start | bytes 7077892
  1.9 16.4 %copy-start.2 = (bf16[64,3072]{1,0:T(8,128)(2,1)S(1)}, bf16[64,3072]{1,0:T(8,128)(2,1)}, u32[]{:S(2)}) copy-start(bf16[64,3072]{1,0:T(8,128)(2,1)} %w_in.1) | copy-start | bytes 1179652
  2.0 16.4 %copy-start.3 = (bf16[3072,64]{0,1:T(8,128)(2,1)S(1)}, bf16[3072,64]{0,1:T(8,128)(2,1)}, u32[]{:S(2)}) copy-start(bf16[3072,64]{0,1:T(8,128)(2,1)} %param.23) | copy-start | bytes 1179652
  18.4 15.1 %copy-start.4 = (f32[16,64]{1,0:T(8,128)S(1)}, f32[16,64]{1,0:T(8,128)}, u32[]{:S(2)}) copy-start(f32[16,64]{1,0:T(8,128)} %param.16) | copy-start | bytes 12292
  18.4 15.1 %copy-start.5 = (f32[1,16,64]{2,1,0:T(8,128)S(1)}, f32[1,16,64]{2,1,0:T(8,128)}, u32[]{:S(2)}) copy-start(f32[1,16,64]{2,1,0:T(8,128)} %latents.1) | copy-start | bytes 12292
  33.4 21.6 %all-to-all-start.4 = ((bf16[16,8,128]{2,1,0:T(8,128)(2,1)}), bf16[16,8,128]{2,1,0:T(8,128)(2,1)S(1)}, u32[]{:S(2)}, u32[]{:S(2)}) async-start(bf16[16,8,128]{2,1,0:T(8,128)(2,1)} %get-tuple-element.54), calls=%async_computation.4 | async-start | bytes 65536 | tf_op jit(solution)/shard_map/all_to_all | solution.py:260

commit v6 on v5

--- a/solution.py
+++ b/solution.py
@@ -15,7 +15,6 @@
 TP = AXES[3:]
 SMEM = pl.BlockSpec(memory_space=pltpu.SMEM)
 VMEM = pl.BlockSpec(memory_space=pltpu.VMEM)
-HBM = pl.BlockSpec(memory_space=pltpu.HBM)
 F32 = jnp.float32
 BF16 = jnp.bfloat16
 
@@ -33,17 +32,6 @@
     )
 
 
-def held(*arrays):
-    return [pltpu.with_memory_space_constraint(a, pltpu.HBM) for a in arrays]
-
-
-def load(pairs, sems):
-    copies = [pltpu.make_async_copy(src, dst, sems.at[i]) for i, (src, dst) in enumerate(pairs)]
-    for copy in copies:
-        copy.start()
-    return copies
-
-
 def fold(rows):
     half = rows.shape[0] // 2
     return jnp.concatenate([rows[:half], rows[half:]], axis=1)
@@ -62,20 +50,19 @@
     return high, value - high
 
 
-def prepare(t_index, dt_units, flag, latents, w_time, *refs):
-    sent, factor, lat_here, w_here, sems = refs
-    copies = load([(w_time, w_here), (latents, lat_here)], sems)
-    half = w_here.shape[1] // 2
-    order = lax.broadcasted_iota(jnp.int32, (16, half), 1).astype(F32)
-    freqs = jnp.exp(-jnp.log(jnp.full((16, half), 10000.0, F32)) * order / half)
-    angle = jnp.full((16, half), t_index[0], jnp.int32).astype(F32) * freqs
+def table(freqs):
+    half = freqs.shape[1]
+    order = lax.broadcasted_iota(jnp.int32, freqs.shape, 1).astype(F32)
+    freqs[...] = jnp.exp(-jnp.log(jnp.full(freqs.shape, 10000.0, F32)) * order / half)
+
+
+def prepare(t_index, dt_units, flag, freqs, latents, w_time, sent, factor):
+    angle = jnp.full(freqs.shape, t_index[0], jnp.int32).astype(F32) * freqs[...]
     emb = jnp.concatenate([jnp.cos(angle), jnp.sin(angle)], axis=1).astype(BF16)
     factor[...] = jnp.full(factor.shape, dt_units[0], jnp.int32).astype(F32) * 0.0078125
-    copies[1].wait()
-    lat = fold(lat_here[0])
-    copies[0].wait()
+    lat = fold(latents[0])
     dims = (((1,), (1,)), ((), ()))
-    mods = lax.dot_general(emb, w_here[...], dims, preferred_element_type=F32)[:1]
+    mods = lax.dot_general(emb, w_time[...], dims, preferred_element_type=F32)[:1]
     gap = jnp.zeros((1, LANES // 2), F32)
     odd = lax.axis_index(TP) % 2 == 1
     mods = jnp.where(odd, jnp.concatenate([gap, mods], 1), jnp.concatenate([mods, gap], 1))
@@ -189,22 +176,24 @@
     hid = w_up.shape[1]
     tokens = tok_rows * devices
     packed = jax.ShapeDtypeStruct((MODS_AT, LANES), F32)
-    w_time_t = w_time.T
     weights = (w_in, w_out.T, w_up, w_down)
 
     early = lax.axis_index("far") == 0
+    flag = early.astype(jnp.int32).reshape(1)
+    freqs = call(
+        table,
+        jax.ShapeDtypeStruct((16, w_time.shape[0] // 2), F32),
+        [],
+        "table",
+        flops=1 << 34,
+    )()
     sent, factor = call(
         prepare,
         [jax.ShapeDtypeStruct((devices, 16, LANES), F32), packed],
-        [SMEM] * 3 + [HBM] * 2,
+        [SMEM] * 3 + [VMEM] * 3,
         "prepare",
         flops=1 << 34,
-        scratch=[
-            pltpu.VMEM(latents.shape, F32),
-            pltpu.VMEM(w_time_t.shape, BF16),
-            pltpu.SemaphoreType.DMA((2,)),
-        ],
-    )(t_index, dt_units, early.astype(jnp.int32).reshape(1), *held(latents, w_time_t))
+    )(t_index, dt_units, flag, freqs, latents, w_time.T)
     got = lax.all_to_all(sent, TP, 0, 0, tiled=True)
     sent = call(
         block,

time: 67 us -> 66 us (0.985)
  Pallas kernels: 6.16 us -> 5.04 us
    pallas_call x1, Pallas kernels: 1.4 us -> 0.26 us  [local(): call(prepare, [jax.ShapeDtypeStruct((devices, 16, LANES), F32), packed],...]
where the time goes in v6:
time: 66 us; the launch traced here: 65.7 us
  blocking collectives  36.9 us (56%)
  starting transfers between devices  13.9 us (21%)
  waiting for transfers between devices  7.76 us (12%)
  Pallas kernels  5.04 us (8%)
  between operations  2.09 us (3%)
    all_to_all x1, blocking collectives, local(): got = lax.all_to_all(sent, TP, 0, 0, tiled=True)  15.1 us
    all_to_all x1, starting transfers between devices, local(): steps = lax.all_to_all(sent, AXES[:2], 0, 0, tiled=True)  13.9 us
    all_to_all x1, blocking collectives, local(): parts = lax.all_to_all(sent, AXES[2:], 0, 0, tiled=True)  11.2 us
    all_to_all x1, blocking collectives, exchange(): totals = lax.all_to_all(errors(steps, devices, 1), TP, 0, 0, tiled=True)  10.7 us
    all_to_all x1, waiting for transfers between devices, local(): steps = lax.all_to_all(sent, AXES[:2], 0, 0, tiled=True)  7.76 us
    pallas_call x1, Pallas kernels, local(): call(block, jax.ShapeDtypeStruct((2, devices, MODS_AT, LANES), F32), [VME...  3.21 us
  transfers between devices with their start and end apart: 1, of which 1 were waited for; matrix products, arithmetic and copies ran while one was open for 0% of the time, Pallas kernels for 0%

profile of v6, /device:TPU:128, one launch (start us, length us, event | category | flops | bytes accessed | tf_op | source)
XLA Modules:
  0.0 65.7 jit_solution(5123213075267977070)
XLA Ops:
  0.6 0.0 copy-start.4
  0.6 0.0 copy-start.6
  2.0 0.0 copy-done.4
  2.0 0.0 copy-done.6
  2.0 0.0 copy-start
  2.0 0.0 copy-start.1
  2.0 0.0 copy-start.2
  2.1 0.0 copy-start.3
  2.1 0.3 prepare.1
  2.3 15.1 %all_to_all.25.got = f32[16,16,128]{2,1,0:T(8,128)S(1)} all-to-all(f32[16,16,128]{2,1,0:T(8,128)S(1)} %get-tuple-element.52), channel_id=1, replica_groups=mesh['far'=4,'near'=4,'core'=2,'y'=4,'x'=4] {'y','x'}, dimensions={0} | all-to-all | bytes 262144 | tf_op jit(solution)/shard_map/all_to_all | solution.py:197
  17.4 0.0 copy-done
  17.4 0.0 copy-done.1
  17.4 0.0 copy-done.2
  17.4 0.0 copy-done.3
  17.5 0.0 copy-start.5
  17.5 3.2 %block.1 = f32[2,16,8,128]{3,2,1,0:T(8,128)S(1)} custom-call(f32[16,16,128]{2,1,0:T(8,128)S(1)} %all_to_all.25.got, f32[8,128]{1,0:T(8,128)S(1)} %get-tuple-element.53.factor, bf16[64,3072]{1,0:T(8,128)(2,1)S(1)} %copy-done.2, bf16[64,3072]{1,0:T(8,128)(2,1)S(1)} %bitcast.11, bf16[3072,384]{1,0:T(8,128)(2,1)S(1)} %copy-done, bf16[384,3072]{1,0:T(8,128)(2,1)S(1)} %copy-done.1), custom_call_target="tpu_custom_call" | custom-call | flops 855638016 | bytes 1048576 | tf_op jit(solution)/shard_map/block/pallas_call | solution.py:198
  20.7 11.2 %all_to_all.26 = f32[32,8,128]{2,1,0:T(8,128)S(1)} all-to-all(f32[32,8,128]{2,1,0:T(8,128)S(1)} %bitcast.9), channel_id=1, replica_groups=mesh['far'=4,'near'=4,'core'=2,'y'=4,'x'=4] {'core','y','x'}, dimensions={0} | all-to-all | bytes 262144 | tf_op jit(solution)/shard_map/all_to_all | solution.py:211
  31.9 0.6 combine.1
  32.5 0.0 copy-done.5
  32.5 13.9 %all-to-all-start.4 = ((bf16[16,8,128]{2,1,0:T(8,128)(2,1)}), bf16[16,8,128]{2,1,0:T(8,128)(2,1)S(1)}, u32[]{:S(2)}, u32[]{:S(2)}) async-start(bf16[16,8,128]{2,1,0:T(8,128)(2,1)} %get-tuple-element.54), calls=%async_computation.4 | async-start | bytes 65536 | tf_op jit(solution)/shard_map/all_to_all | solution.py:249
  46.4 7.8 %all-to-all-done.4 = bf16[16,8,128]{2,1,0:T(8,128)(2,1)S(1)} async-done(((bf16[16,8,128]{2,1,0:T(8,128)(2,1)}), bf16[16,8,128]{2,1,0:T(8,128)(2,1)S(1)}, u32[]{:S(2)}, u32[]{:S(2)}) %all-to-all-start.4) | async-done | bytes 32800 | tf_op jit(solution)/shard_map/all_to_all | solution.py:249
  54.1 11.6 %conditional.5 = ((f32[1,16,64]{2,1,0:T(8,128)}, f32[1]{0:T(128)})) conditional(s32[]{:T(128)} %convert_element_type.2, (bf16[16,8,128]{2,1,0:T(8,128)(2,1)S(1)}, f32[8,128]{1,0:T(8,128)S(1)}, f32[16,64]{1,0:T(8,128)S(1)}, f32[1,16,64]{2,1,0:T(8,128)S(1)}) %tuple.44, (f32[4,1,128]{2,1,0:T(1,128)S(1)}, bf16[16,8,128]{2,1,0:T(8,128)(2,1)S(1)}, ...), branch_computations={%region_5.0_spmd, %region_6.0_spmd} | conditional | bytes 2113544 | solution.py:251
  54.1 0.2 judge.3
  54.4 10.7 %all_to_all.24.parts = f32[16,1,128]{2,1,0:T(1,128)S(1)} all-to-all(f32[16,1,128]{2,1,0:T(1,128)S(1)} %judge.3), channel_id=1, replica_groups=mesh['far'=4,'near'=4,'core'=2,'y'=4,'x'=4] {'y','x'}, dimensions={0} | all-to-all | bytes 16384 | tf_op jit(solution)/shard_map/cond/branch_0_fun/all_to_all | solution.py:245
  65.0 0.7 %finish.2 = (f32[1,16,64]{2,1,0:T(8,128)}, f32[1]{0:T(128)}) custom-call(f32[16,1,128]{2,1,0:T(1,128)S(1)} %all_to_all.24.parts, bf16[16,8,128]{2,1,0:T(8,128)(2,1)S(1)} %get-tuple-element.37.steps, f32[8,128]{1,0:T(8,128)S(1)} %get-tuple-element.38.first, f32[16,64]{1,0:T(8,128)S(1)} %get-tuple-element.39.start_latent), custom_call_target="tpu_custom_call" | custom-call | bytes 1048576 | tf_op jit(solution)/shard_map/cond/branch_0_fun/finish/pallas_call | solution.py:236
  (5 shorter events, 0.0 us)
Async XLA Ops:
  0.6 1.4 %copy-start.4 = (bf16[256,576]{0,1:T(8,128)(2,1)S(1)}, bf16[256,576]{0,1:T(8,128)(2,1)}, u32[]{:S(2)}) copy-start(bf16[256,576]{0,1:T(8,128)(2,1)} %param.19) | copy-start | bytes 884740
  0.6 1.4 %copy-start.6 = (f32[1,16,64]{2,1,0:T(8,128)S(1)}, f32[1,16,64]{2,1,0:T(8,128)}, u32[]{:S(2)}) copy-start(f32[1,16,64]{2,1,0:T(8,128)} %latents.1) | copy-start | bytes 12292
  2.0 15.4 %copy-start = (bf16[3072,384]{1,0:T(8,128)(2,1)S(1)}, bf16[3072,384]{1,0:T(8,128)(2,1)}, u32[]{:S(2)}) copy-start(bf16[3072,384]{1,0:T(8,128)(2,1)} %w_up.1) | copy-start | bytes 7077892
  2.0 15.4 %copy-start.1 = (bf16[384,3072]{1,0:T(8,128)(2,1)S(1)}, bf16[384,3072]{1,0:T(8,128)(2,1)}, u32[]{:S(2)}) copy-start(bf16[384,3072]{1,0:T(8,128)(2,1)} %w_down.1) | copy-start | bytes 7077892
  2.0 15.4 %copy-start.2 = (bf16[64,3072]{1,0:T(8,128)(2,1)S(1)}, bf16[64,3072]{1,0:T(8,128)(2,1)}, u32[]{:S(2)}) copy-start(bf16[64,3072]{1,0:T(8,128)(2,1)} %w_in.1) | copy-start | bytes 1179652
  2.1 15.4 %copy-start.3 = (bf16[3072,64]{0,1:T(8,128)(2,1)S(1)}, bf16[3072,64]{0,1:T(8,128)(2,1)}, u32[]{:S(2)}) copy-start(bf16[3072,64]{0,1:T(8,128)(2,1)} %param.23) | copy-start | bytes 1179652
  17.5 15.0 %copy-start.5 = (f32[16,64]{1,0:T(8,128)S(1)}, f32[16,64]{1,0:T(8,128)}, u32[]{:S(2)}) copy-start(f32[16,64]{1,0:T(8,128)} %param.16) | copy-start | bytes 12292
  32.5 21.6 %all-to-all-start.4 = ((bf16[16,8,128]{2,1,0:T(8,128)(2,1)}), bf16[16,8,128]{2,1,0:T(8,128)(2,1)S(1)}, u32[]{:S(2)}, u32[]{:S(2)}) async-start(bf16[16,8,128]{2,1,0:T(8,128)(2,1)} %get-tuple-element.54), calls=%async_computation.4 | async-start | bytes 65536 | tf_op jit(solution)/shard_map/all_to_all | solution.py:249

commit v7 on v6

--- a/solution.py
+++ b/solution.py
@@ -130,16 +130,16 @@
     part = part.reshape(devices, MODS_AT, LANES)
     mine = lax.broadcasted_iota(jnp.int32, part.shape, 0) == lax.axis_index(TP)
     part = jnp.where(mine, part + own[None], part) * factor[...][None]
-    sent[0] = part
-    sent[1] = part
+    sent[0] = part.astype(BF16)
+    sent[1] = part.astype(BF16)
 
 
 def combine(parts, sent, near, first):
-    one = parts[0, 0]
-    two = parts[1, 0]
+    one = parts[0, 0].astype(F32)
+    two = parts[1, 0].astype(F32)
     for device in range(1, parts.shape[1]):
-        one = one + parts[0, device]
-        two = two + parts[1, device]
+        one = one + parts[0, device].astype(F32)
+        two = two + parts[1, device].astype(F32)
     first[...] = one
     both = (one + two).astype(BF16)
     for device in range(sent.shape[0]):
@@ -197,7 +197,7 @@
     got = lax.all_to_all(sent, TP, 0, 0, tiled=True)
     sent = call(
         block,
-        jax.ShapeDtypeStruct((2, devices, MODS_AT, LANES), F32),
+        jax.ShapeDtypeStruct((2, devices, MODS_AT, LANES), BF16),
         [VMEM] * 6,
         "block",
         flops=2 * tokens * width * (hid + channels) + 2 * hid * width * channels,

time: 66 us -> 65.6 us (level)
  no operation moved by 1% of the time
where the time goes in v7:
time: 65.6 us; the launch traced here: 65.3 us
  blocking collectives  36.5 us (56%)
  starting transfers between devices  13.9 us (21%)
  waiting for transfers between devices  7.76 us (12%)
  Pallas kernels  5.04 us (8%)
  between operations  2.09 us (3%)
    all_to_all x1, blocking collectives, local(): got = lax.all_to_all(sent, TP, 0, 0, tiled=True)  15.1 us
    all_to_all x1, starting transfers between devices, local(): steps = lax.all_to_all(sent, AXES[:2], 0, 0, tiled=True)  13.9 us
    all_to_all x1, blocking collectives, local(): parts = lax.all_to_all(sent, AXES[2:], 0, 0, tiled=True)  10.8 us
    all_to_all x1, blocking collectives, exchange(): totals = lax.all_to_all(errors(steps, devices, 1), TP, 0, 0, tiled=True)  10.6 us
    all_to_all x1, waiting for transfers between devices, local(): steps = lax.all_to_all(sent, AXES[:2], 0, 0, tiled=True)  7.76 us
    pallas_call x1, Pallas kernels, local(): call(block, jax.ShapeDtypeStruct((2, devices, MODS_AT, LANES), BF16), [VM...  3.21 us
  transfers between devices with their start and end apart: 1, of which 1 were waited for; matrix products, arithmetic and copies ran while one was open for 0% of the time, Pallas kernels for 0%

profile of v7, /device:TPU:128, one launch (start us, length us, event | category | flops | bytes accessed | tf_op | source)
XLA Modules:
  0.0 65.3 jit_solution(13226452064398290817)
XLA Ops:
  0.6 0.0 copy-start.4
  0.6 0.0 copy-start.6
  2.0 0.0 copy-done.4
  2.0 0.0 copy-done.6
  2.0 0.0 copy-start
  2.0 0.0 copy-start.1
  2.0 0.0 copy-start.2
  2.1 0.0 copy-start.3
  2.1 0.3 prepare.1
  2.3 15.1 %all_to_all.25.got = f32[16,16,128]{2,1,0:T(8,128)S(1)} all-to-all(f32[16,16,128]{2,1,0:T(8,128)S(1)} %get-tuple-element.52), channel_id=1, replica_groups=mesh['far'=4,'near'=4,'core'=2,'y'=4,'x'=4] {'y','x'}, dimensions={0} | all-to-all | bytes 262144 | tf_op jit(solution)/shard_map/all_to_all | solution.py:197
  17.4 0.0 copy-done
  17.4 0.0 copy-done.1
  17.4 0.0 copy-done.2
  17.4 0.0 copy-done.3
  17.5 0.0 copy-start.5
  17.5 3.2 %block.1 = bf16[2,16,8,128]{3,2,1,0:T(8,128)(2,1)S(1)} custom-call(f32[16,16,128]{2,1,0:T(8,128)S(1)} %all_to_all.25.got, f32[8,128]{1,0:T(8,128)S(1)} %get-tuple-element.53.factor, bf16[64,3072]{1,0:T(8,128)(2,1)S(1)} %copy-done.2, bf16[64,3072]{1,0:T(8,128)(2,1)S(1)} %bitcast.9, bf16[3072,384]{1,0:T(8,128)(2,1)S(1)} %copy-done, bf16[384,3072]{1,0:T(8,128)(2,1)S(1)} %copy-done.1), custom_call_target="tpu_custom_call" | custom-call | flops 855638016 | bytes 1048576 | tf_op jit(solution)/shard_map/block/pallas_call | solution.py:198
  20.7 10.8 %all_to_all.26 = bf16[32,8,128]{2,1,0:T(8,128)(2,1)S(1)} all-to-all(bf16[32,8,128]{2,1,0:T(8,128)(2,1)S(1)} %bitcast.10), channel_id=1, replica_groups=mesh['far'=4,'near'=4,'core'=2,'y'=4,'x'=4] {'core','y','x'}, dimensions={0} | all-to-all | bytes 131072 | tf_op jit(solution)/shard_map/all_to_all | solution.py:211
  31.5 0.6 combine.1
  32.1 0.0 copy-done.5
  32.1 13.9 %all-to-all-start.4 = ((bf16[16,8,128]{2,1,0:T(8,128)(2,1)}), bf16[16,8,128]{2,1,0:T(8,128)(2,1)S(1)}, u32[]{:S(2)}, u32[]{:S(2)}) async-start(bf16[16,8,128]{2,1,0:T(8,128)(2,1)} %get-tuple-element.54), calls=%async_computation.4 | async-start | bytes 65536 | tf_op jit(solution)/shard_map/all_to_all | solution.py:249
  46.0 7.8 %all-to-all-done.4 = bf16[16,8,128]{2,1,0:T(8,128)(2,1)S(1)} async-done(((bf16[16,8,128]{2,1,0:T(8,128)(2,1)}), bf16[16,8,128]{2,1,0:T(8,128)(2,1)S(1)}, u32[]{:S(2)}, u32[]{:S(2)}) %all-to-all-start.4) | async-done | bytes 32800 | tf_op jit(solution)/shard_map/all_to_all | solution.py:249
  53.8 11.6 %conditional.5 = ((f32[1,16,64]{2,1,0:T(8,128)}, f32[1]{0:T(128)})) conditional(s32[]{:T(128)} %convert_element_type.2, (bf16[16,8,128]{2,1,0:T(8,128)(2,1)S(1)}, f32[8,128]{1,0:T(8,128)S(1)}, f32[16,64]{1,0:T(8,128)S(1)}, f32[1,16,64]{2,1,0:T(8,128)S(1)}) %tuple.44, (f32[4,1,128]{2,1,0:T(1,128)S(1)}, bf16[16,8,128]{2,1,0:T(8,128)(2,1)S(1)}, ...), branch_computations={%region_5.0_spmd, %region_6.0_spmd} | conditional | bytes 2113544 | solution.py:251
  53.8 0.2 judge.3
  54.0 10.6 %all_to_all.24.parts = f32[16,1,128]{2,1,0:T(1,128)S(1)} all-to-all(f32[16,1,128]{2,1,0:T(1,128)S(1)} %judge.3), channel_id=1, replica_groups=mesh['far'=4,'near'=4,'core'=2,'y'=4,'x'=4] {'y','x'}, dimensions={0} | all-to-all | bytes 16384 | tf_op jit(solution)/shard_map/cond/branch_0_fun/all_to_all | solution.py:245
  64.6 0.7 %finish.2 = (f32[1,16,64]{2,1,0:T(8,128)}, f32[1]{0:T(128)}) custom-call(f32[16,1,128]{2,1,0:T(1,128)S(1)} %all_to_all.24.parts, bf16[16,8,128]{2,1,0:T(8,128)(2,1)S(1)} %get-tuple-element.37.steps, f32[8,128]{1,0:T(8,128)S(1)} %get-tuple-element.38.first, f32[16,64]{1,0:T(8,128)S(1)} %get-tuple-element.39.start_latent), custom_call_target="tpu_custom_call" | custom-call | bytes 1048576 | tf_op jit(solution)/shard_map/cond/branch_0_fun/finish/pallas_call | solution.py:236
  (5 shorter events, 0.0 us)
Async XLA Ops:
  0.6 1.4 %copy-start.4 = (bf16[256,576]{0,1:T(8,128)(2,1)S(1)}, bf16[256,576]{0,1:T(8,128)(2,1)}, u32[]{:S(2)}) copy-start(bf16[256,576]{0,1:T(8,128)(2,1)} %param.19) | copy-start | bytes 884740
  0.6 1.4 %copy-start.6 = (f32[1,16,64]{2,1,0:T(8,128)S(1)}, f32[1,16,64]{2,1,0:T(8,128)}, u32[]{:S(2)}) copy-start(f32[1,16,64]{2,1,0:T(8,128)} %latents.1) | copy-start | bytes 12292
  2.0 15.4 %copy-start = (bf16[3072,384]{1,0:T(8,128)(2,1)S(1)}, bf16[3072,384]{1,0:T(8,128)(2,1)}, u32[]{:S(2)}) copy-start(bf16[3072,384]{1,0:T(8,128)(2,1)} %w_up.1) | copy-start | bytes 7077892
  2.0 15.4 %copy-start.1 = (bf16[384,3072]{1,0:T(8,128)(2,1)S(1)}, bf16[384,3072]{1,0:T(8,128)(2,1)}, u32[]{:S(2)}) copy-start(bf16[384,3072]{1,0:T(8,128)(2,1)} %w_down.1) | copy-start | bytes 7077892
  2.0 15.4 %copy-start.2 = (bf16[64,3072]{1,0:T(8,128)(2,1)S(1)}, bf16[64,3072]{1,0:T(8,128)(2,1)}, u32[]{:S(2)}) copy-start(bf16[64,3072]{1,0:T(8,128)(2,1)} %w_in.1) | copy-start | bytes 1179652
  2.1 15.4 %copy-start.3 = (bf16[3072,64]{0,1:T(8,128)(2,1)S(1)}, bf16[3072,64]{0,1:T(8,128)(2,1)}, u32[]{:S(2)}) copy-start(bf16[3072,64]{0,1:T(8,128)(2,1)} %param.23) | copy-start | bytes 1179652
  17.5 14.7 %copy-start.5 = (f32[16,64]{1,0:T(8,128)S(1)}, f32[16,64]{1,0:T(8,128)}, u32[]{:S(2)}) copy-start(f32[16,64]{1,0:T(8,128)} %param.16) | copy-start | bytes 12292
  32.1 21.6 %all-to-all-start.4 = ((bf16[16,8,128]{2,1,0:T(8,128)(2,1)}), bf16[16,8,128]{2,1,0:T(8,128)(2,1)S(1)}, u32[]{:S(2)}, u32[]{:S(2)}) async-start(bf16[16,8,128]{2,1,0:T(8,128)(2,1)} %get-tuple-element.54), calls=%async_computation.4 | async-start | bytes 65536 | tf_op jit(solution)/shard_map/all_to_all | solution.py:249

commit v8 on v7

--- a/solution.py
+++ b/solution.py
@@ -97,29 +97,34 @@
     lat = jnp.concatenate([lat[:, : LANES // 2], lat[:, LANES // 2 :]], axis=0).astype(BF16)
     tokens = lat.shape[0]
     step = 512
+    columns = w_in[:, :LANES].astype(F32)
+    for start in range(LANES, width, LANES):
+        columns = columns + w_in[:, start : start + LANES].astype(F32)
+    high, low = split(columns)
+    rest, last = split(low)
+    columns = jnp.concatenate([high, rest, last], axis=1).astype(BF16)
+    total = jnp.dot(lat, columns, preferred_element_type=F32)
+    total = total[:, :LANES] + (total[:, LANES : 2 * LANES] + total[:, 2 * LANES :])
+    mean = jnp.sum(total, axis=1, keepdims=True) / width
     total = jnp.zeros((tokens, LANES), F32)
     for start in range(0, width, step):
-        part = jnp.dot(lat, w_in[:, start : start + step], preferred_element_type=F32)
-        hidden[:, start : start + step] = part
+        center = jnp.dot(lat, w_in[:, start : start + step], preferred_element_type=F32) - mean
+        hidden[:, start : start + step] = center
         for at in range(0, step, LANES):
-            total = total + part[:, at : at + LANES]
-    place = pl.multiple_of(lax.axis_index(TP) * MODS_AT, MODS_AT)
-    own = [hidden[pl.ds(place + at, MODS_AT), :] for at in (0, tokens // 2)]
-    high, low = split(jnp.concatenate(own, axis=0))
+            total = total + center[:, at : at + LANES] * center[:, at : at + LANES]
+
+    own = got[lax.axis_index(TP), :MODS_AT, :]
+    own = jnp.concatenate([own[:, : LANES // 2], own[:, LANES // 2 :]], axis=0).astype(BF16)
+    high, low = split(jnp.dot(own, w_in[...], preferred_element_type=F32))
     rest, last = split(low)
     own = jnp.concatenate([high, rest, last], axis=0).astype(BF16)
     own = lax.dot_general(own, w_out_t[...], dims, preferred_element_type=F32)
     own = fold(own[:16] + own[16:32] + own[32:48])
-    mean = jnp.sum(total, axis=1, keepdims=True) / width
-    total = jnp.zeros((tokens, LANES), F32)
-    for start in range(0, width, LANES):
-        center = hidden[:, start : start + LANES] - mean
-        total = total + center * center
     spread = jnp.sum(total, axis=1, keepdims=True) / width
     inverse = 1.0 / jnp.sqrt(spread + 1e-06)
     for i in range(count):
         at = slice(i * LANES, (i + 1) * LANES)
-        value = (hidden[:, at] - mean) * inverse * (1.0 + scale[i]) + shift[i]
+        value = hidden[:, at] * inverse * (1.0 + scale[i]) + shift[i]
         normed[:, at] = value.astype(BF16)
     up = jnp.dot(normed[...], w_up[...], preferred_element_type=F32)
     act = jax.nn.gelu(up, approximate=True).astype(BF16)
@@ -148,25 +153,27 @@
         near[device] = both
 
 
-def advance(steps, first, start_latent):
-    before = jnp.where(lax.axis_index("core") == 1, first[...], 0.0)
+def before(steps, first):
+    total = jnp.where(lax.axis_index("core") == 1, first[...], 0.0)
     here = lax.axis_index(AXES[:2])
     for z in range(steps.shape[0]):
-        before = before + jnp.where(z < here, steps[z].astype(F32), 0.0)
+        total = total + jnp.where(z < here, steps[z].astype(F32), 0.0)
+    return total
+
+
+def judge(steps, first, start_latent, latents, sent):
+    change = fold(start_latent[...] - latents[0]) + before(steps, first)
+    count = change.size * lax.axis_size(TP)
+    part = jnp.sum(change * change, axis=0, keepdims=True) / count
+    sent[...] = jnp.broadcast_to(part, sent.shape)
+
+
+def finish(parts, steps, first, start_latent, new_latents, step_error):
     half = LANES // 2
-    before = jnp.concatenate([before[:, :half], before[:, half:]], axis=0)
-    return start_latent[...] + before
-
-
-def judge(steps, first, start_latent, latents, sent):
-    change = advance(steps, first, start_latent) - latents[0]
-    count = change.size * lax.axis_size(TP)
-    sent[...] = jnp.full(sent.shape, jnp.sum(change * change) / count, F32)
-
-
-def finish(parts, steps, first, start_latent, new_latents, step_error):
-    new_latents[0] = advance(steps, first, start_latent)
-    step_error[0] = jnp.sum(parts[...], axis=0)[0, 0]
+    change = before(steps, first)
+    change = jnp.concatenate([change[:, :half], change[:, half:]], axis=0)
+    new_latents[0] = start_latent[...] + change
+    step_error[0] = jnp.sum(parts[...])
 
 
 def local(latents, start_latent, t_index, dt_units, w_time, w_in, w_up, w_down, w_out):

time: 65.6 us -> 65.1 us (level)
  no operation moved by 1% of the time
where the time goes in v8:
time: 65.1 us; the launch traced here: 64.8 us
  blocking collectives  36.5 us (56%)
  starting transfers between devices  13.8 us (21%)
  waiting for transfers between devices  7.76 us (12%)
  Pallas kernels  4.55 us (7%)
  between operations  2.09 us (3%)
    all_to_all x1, blocking collectives, local(): got = lax.all_to_all(sent, TP, 0, 0, tiled=True)  15.1 us
    all_to_all x1, starting transfers between devices, local(): steps = lax.all_to_all(sent, AXES[:2], 0, 0, tiled=True)  13.8 us
    all_to_all x1, blocking collectives, local(): parts = lax.all_to_all(sent, AXES[2:], 0, 0, tiled=True)  10.8 us
    all_to_all x1, blocking collectives, exchange(): totals = lax.all_to_all(errors(steps, devices, 1), TP, 0, 0, tiled=True)  10.6 us
    all_to_all x1, waiting for transfers between devices, local(): steps = lax.all_to_all(sent, AXES[:2], 0, 0, tiled=True)  7.76 us
    pallas_call x1, Pallas kernels, local(): call(block, jax.ShapeDtypeStruct((2, devices, MODS_AT, LANES), BF16), [VM...  2.85 us
  transfers between devices with their start and end apart: 1, of which 1 were waited for; matrix products, arithmetic and copies ran while one was open for 0% of the time, Pallas kernels for 0%

profile of v8, /device:TPU:128, one launch (start us, length us, event | category | flops | bytes accessed | tf_op | source)
XLA Modules:
  0.0 64.8 jit_solution(600556917204219108)
XLA Ops:
  0.6 0.0 copy-start.4
  0.6 0.0 copy-start.6
  2.0 0.0 copy-done.4
  2.0 0.0 copy-done.6
  2.0 0.0 copy-start
  2.0 0.0 copy-start.1
  2.0 0.0 copy-start.2
  2.1 0.0 copy-start.3
  2.1 0.3 prepare.1
  2.3 15.1 %all_to_all.25.got = f32[16,16,128]{2,1,0:T(8,128)S(1)} all-to-all(f32[16,16,128]{2,1,0:T(8,128)S(1)} %get-tuple-element.52), channel_id=1, replica_groups=mesh['far'=4,'near'=4,'core'=2,'y'=4,'x'=4] {'y','x'}, dimensions={0} | all-to-all | bytes 262144 | tf_op jit(solution)/shard_map/all_to_all | solution.py:204
  17.4 0.0 copy-done
  17.4 0.0 copy-done.1
  17.4 0.0 copy-done.2
  17.4 0.0 copy-done.3
  17.5 0.0 copy-start.5
  17.5 2.8 %block.1 = bf16[2,16,8,128]{3,2,1,0:T(8,128)(2,1)S(1)} custom-call(f32[16,16,128]{2,1,0:T(8,128)S(1)} %all_to_all.25.got, f32[8,128]{1,0:T(8,128)S(1)} %get-tuple-element.53.factor, bf16[64,3072]{1,0:T(8,128)(2,1)S(1)} %copy-done.2, bf16[64,3072]{1,0:T(8,128)(2,1)S(1)} %bitcast.9, bf16[3072,384]{1,0:T(8,128)(2,1)S(1)} %copy-done, bf16[384,3072]{1,0:T(8,128)(2,1)S(1)} %copy-done.1), custom_call_target="tpu_custom_call" | custom-call | flops 855638016 | bytes 1048576 | tf_op jit(solution)/shard_map/block/pallas_call | solution.py:205
  20.3 10.8 %all_to_all.26 = bf16[32,8,128]{2,1,0:T(8,128)(2,1)S(1)} all-to-all(bf16[32,8,128]{2,1,0:T(8,128)(2,1)S(1)} %bitcast.10), channel_id=1, replica_groups=mesh['far'=4,'near'=4,'core'=2,'y'=4,'x'=4] {'core','y','x'}, dimensions={0} | all-to-all | bytes 131072 | tf_op jit(solution)/shard_map/all_to_all | solution.py:218
  31.1 0.6 combine.1
  31.8 0.0 copy-done.5
  31.8 13.8 %all-to-all-start.4 = ((bf16[16,8,128]{2,1,0:T(8,128)(2,1)}), bf16[16,8,128]{2,1,0:T(8,128)(2,1)S(1)}, u32[]{:S(2)}, u32[]{:S(2)}) async-start(bf16[16,8,128]{2,1,0:T(8,128)(2,1)} %get-tuple-element.54), calls=%async_computation.4 | async-start | bytes 65536 | tf_op jit(solution)/shard_map/all_to_all | solution.py:256
  45.6 7.8 %all-to-all-done.4 = bf16[16,8,128]{2,1,0:T(8,128)(2,1)S(1)} async-done(((bf16[16,8,128]{2,1,0:T(8,128)(2,1)}), bf16[16,8,128]{2,1,0:T(8,128)(2,1)S(1)}, u32[]{:S(2)}, u32[]{:S(2)}) %all-to-all-start.4) | async-done | bytes 32800 | tf_op jit(solution)/shard_map/all_to_all | solution.py:256
  53.4 11.4 %conditional.5 = ((f32[1,16,64]{2,1,0:T(8,128)}, f32[1]{0:T(128)})) conditional(s32[]{:T(128)} %convert_element_type.2, (bf16[16,8,128]{2,1,0:T(8,128)(2,1)S(1)}, f32[8,128]{1,0:T(8,128)S(1)}, f32[16,64]{1,0:T(8,128)S(1)}, f32[1,16,64]{2,1,0:T(8,128)S(1)}) %tuple.44, (f32[4,1,128]{2,1,0:T(1,128)S(1)}, bf16[16,8,128]{2,1,0:T(8,128)(2,1)S(1)}, ...), branch_computations={%region_5.0_spmd, %region_6.0_spmd} | conditional | bytes 2113544 | solution.py:258
  53.4 0.1 judge.3
  53.5 10.6 %all_to_all.24.parts = f32[16,1,128]{2,1,0:T(1,128)S(1)} all-to-all(f32[16,1,128]{2,1,0:T(1,128)S(1)} %judge.3), channel_id=1, replica_groups=mesh['far'=4,'near'=4,'core'=2,'y'=4,'x'=4] {'y','x'}, dimensions={0} | all-to-all | bytes 16384 | tf_op jit(solution)/shard_map/cond/branch_0_fun/all_to_all | solution.py:252
  64.1 0.7 %finish.2 = (f32[1,16,64]{2,1,0:T(8,128)}, f32[1]{0:T(128)}) custom-call(f32[16,1,128]{2,1,0:T(1,128)S(1)} %all_to_all.24.parts, bf16[16,8,128]{2,1,0:T(8,128)(2,1)S(1)} %get-tuple-element.37.steps, f32[8,128]{1,0:T(8,128)S(1)} %get-tuple-element.38.first, f32[16,64]{1,0:T(8,128)S(1)} %get-tuple-element.39.start_latent), custom_call_target="tpu_custom_call" | custom-call | bytes 1048576 | tf_op jit(solution)/shard_map/cond/branch_0_fun/finish/pallas_call | solution.py:243
  (5 shorter events, 0.0 us)
Async XLA Ops:
  0.6 1.4 %copy-start.4 = (bf16[256,576]{0,1:T(8,128)(2,1)S(1)}, bf16[256,576]{0,1:T(8,128)(2,1)}, u32[]{:S(2)}) copy-start(bf16[256,576]{0,1:T(8,128)(2,1)} %param.19) | copy-start | bytes 884740
  0.6 1.4 %copy-start.6 = (f32[1,16,64]{2,1,0:T(8,128)S(1)}, f32[1,16,64]{2,1,0:T(8,128)}, u32[]{:S(2)}) copy-start(f32[1,16,64]{2,1,0:T(8,128)} %latents.1) | copy-start | bytes 12292
  2.0 15.4 %copy-start = (bf16[3072,384]{1,0:T(8,128)(2,1)S(1)}, bf16[3072,384]{1,0:T(8,128)(2,1)}, u32[]{:S(2)}) copy-start(bf16[3072,384]{1,0:T(8,128)(2,1)} %w_up.1) | copy-start | bytes 7077892
  2.0 15.4 %copy-start.1 = (bf16[384,3072]{1,0:T(8,128)(2,1)S(1)}, bf16[384,3072]{1,0:T(8,128)(2,1)}, u32[]{:S(2)}) copy-start(bf16[384,3072]{1,0:T(8,128)(2,1)} %w_down.1) | copy-start | bytes 7077892
  2.0 15.4 %copy-start.2 = (bf16[64,3072]{1,0:T(8,128)(2,1)S(1)}, bf16[64,3072]{1,0:T(8,128)(2,1)}, u32[]{:S(2)}) copy-start(bf16[64,3072]{1,0:T(8,128)(2,1)} %w_in.1) | copy-start | bytes 1179652
  2.1 15.4 %copy-start.3 = (bf16[3072,64]{0,1:T(8,128)(2,1)S(1)}, bf16[3072,64]{0,1:T(8,128)(2,1)}, u32[]{:S(2)}) copy-start(bf16[3072,64]{0,1:T(8,128)(2,1)} %param.23) | copy-start | bytes 1179652
  17.5 14.3 %copy-start.5 = (f32[16,64]{1,0:T(8,128)S(1)}, f32[16,64]{1,0:T(8,128)}, u32[]{:S(2)}) copy-start(f32[16,64]{1,0:T(8,128)} %param.16) | copy-start | bytes 12292
  31.8 21.6 %all-to-all-start.4 = ((bf16[16,8,128]{2,1,0:T(8,128)(2,1)}), bf16[16,8,128]{2,1,0:T(8,128)(2,1)S(1)}, u32[]{:S(2)}, u32[]{:S(2)}) async-start(bf16[16,8,128]{2,1,0:T(8,128)(2,1)} %get-tuple-element.54), calls=%async_computation.4 | async-start | bytes 65536 | tf_op jit(solution)/shard_map/all_to_all | solution.py:256

commit v9 on v8

--- a/solution.py
+++ b/solution.py
@@ -50,7 +50,8 @@
     return high, value - high
 
 
-def table(freqs):
+def table(freqs, early):
+    early[0] = (lax.axis_index("far") == 0).astype(jnp.int32)
     half = freqs.shape[1]
     order = lax.broadcasted_iota(jnp.int32, freqs.shape, 1).astype(F32)
     freqs[...] = jnp.exp(-jnp.log(jnp.full(freqs.shape, 10000.0, F32)) * order / half)
@@ -185,15 +186,19 @@
     packed = jax.ShapeDtypeStruct((MODS_AT, LANES), F32)
     weights = (w_in, w_out.T, w_up, w_down)
 
-    early = lax.axis_index("far") == 0
-    flag = early.astype(jnp.int32).reshape(1)
-    freqs = call(
+    freqs, early = call(
         table,
-        jax.ShapeDtypeStruct((16, w_time.shape[0] // 2), F32),
+        (
+            jax.ShapeDtypeStruct((16, w_time.shape[0] // 2), F32),
+            pltpu.SMEM((1,), jnp.int32),
+        ),
         [],
         "table",
         flops=1 << 34,
+        out_specs=(VMEM, SMEM),
     )()
+    early = early[0] != 0
+    flag = early.astype(jnp.int32).reshape(1)
     sent, factor = call(
         prepare,
         [jax.ShapeDtypeStruct((devices, 16, LANES), F32), packed],

time: 65.1 us -> 65.1 us (level)
  no operation moved by 1% of the time
where the time goes in v9:
time: 65.1 us; the launch traced here: 64.8 us
  blocking collectives  36.5 us (56%)
  starting transfers between devices  13.8 us (21%)
  waiting for transfers between devices  7.76 us (12%)
  Pallas kernels  4.54 us (7%)
  between operations  2.09 us (3%)
    all_to_all x1, blocking collectives, local(): got = lax.all_to_all(sent, TP, 0, 0, tiled=True)  15.1 us
    all_to_all x1, starting transfers between devices, local(): steps = lax.all_to_all(sent, AXES[:2], 0, 0, tiled=True)  13.8 us
    all_to_all x1, blocking collectives, local(): parts = lax.all_to_all(sent, AXES[2:], 0, 0, tiled=True)  10.8 us
    all_to_all x1, blocking collectives, exchange(): totals = lax.all_to_all(errors(steps, devices, 1), TP, 0, 0, tiled=True)  10.6 us
    all_to_all x1, waiting for transfers between devices, local(): steps = lax.all_to_all(sent, AXES[:2], 0, 0, tiled=True)  7.76 us
    pallas_call x1, Pallas kernels, local(): call(block, jax.ShapeDtypeStruct((2, devices, MODS_AT, LANES), BF16), [VM...  2.85 us
  transfers between devices with their start and end apart: 1, of which 1 were waited for; matrix products, arithmetic and copies ran while one was open for 0% of the time, Pallas kernels for 0%

profile of v9, /device:TPU:128, one launch (start us, length us, event | category | flops | bytes accessed | tf_op | source)
XLA Modules:
  0.0 64.8 jit_solution(4371997069842795272)
XLA Ops:
  0.6 0.0 copy-start.6
  0.6 0.0 copy-start.4
  2.0 0.0 copy-done.6
  2.0 0.0 copy-done.4
  2.0 0.0 copy-start
  2.0 0.0 copy-start.1
  2.1 0.0 copy-start.2
  2.1 0.0 copy-start.3
  2.1 0.3 prepare.1
  2.4 15.1 %all_to_all.25.got = f32[16,16,128]{2,1,0:T(8,128)S(1)} all-to-all(f32[16,16,128]{2,1,0:T(8,128)S(1)} %get-tuple-element.56), channel_id=1, replica_groups=mesh['far'=4,'near'=4,'core'=2,'y'=4,'x'=4] {'y','x'}, dimensions={0} | all-to-all | bytes 262144 | tf_op jit(solution)/shard_map/all_to_all | solution.py:209
  17.4 0.0 copy-done
  17.4 0.0 copy-done.1
  17.4 0.0 copy-done.2
  17.5 0.0 copy-done.3
  17.5 0.0 copy-start.5
  17.5 2.8 %block.1 = bf16[2,16,8,128]{3,2,1,0:T(8,128)(2,1)S(1)} custom-call(f32[16,16,128]{2,1,0:T(8,128)S(1)} %all_to_all.25.got, f32[8,128]{1,0:T(8,128)S(1)} %get-tuple-element.57.factor, bf16[64,3072]{1,0:T(8,128)(2,1)S(1)} %copy-done.2, bf16[64,3072]{1,0:T(8,128)(2,1)S(1)} %bitcast.9, bf16[3072,384]{1,0:T(8,128)(2,1)S(1)} %copy-done, bf16[384,3072]{1,0:T(8,128)(2,1)S(1)} %copy-done.1), custom_call_target="tpu_custom_call" | custom-call | flops 855638016 | bytes 1048576 | tf_op jit(solution)/shard_map/block/pallas_call | solution.py:210
  20.3 10.8 %all_to_all.26 = bf16[32,8,128]{2,1,0:T(8,128)(2,1)S(1)} all-to-all(bf16[32,8,128]{2,1,0:T(8,128)(2,1)S(1)} %bitcast.10), channel_id=1, replica_groups=mesh['far'=4,'near'=4,'core'=2,'y'=4,'x'=4] {'core','y','x'}, dimensions={0} | all-to-all | bytes 131072 | tf_op jit(solution)/shard_map/all_to_all | solution.py:223
  31.2 0.6 combine.1
  31.8 0.0 copy-done.5
  31.8 13.8 %all-to-all-start.4 = ((bf16[16,8,128]{2,1,0:T(8,128)(2,1)}), bf16[16,8,128]{2,1,0:T(8,128)(2,1)S(1)}, u32[]{:S(2)}, u32[]{:S(2)}) async-start(bf16[16,8,128]{2,1,0:T(8,128)(2,1)} %get-tuple-element.58), calls=%async_computation.4 | async-start | bytes 65536 | tf_op jit(solution)/shard_map/all_to_all | solution.py:261
  45.6 7.8 %all-to-all-done.4 = bf16[16,8,128]{2,1,0:T(8,128)(2,1)S(1)} async-done(((bf16[16,8,128]{2,1,0:T(8,128)(2,1)}), bf16[16,8,128]{2,1,0:T(8,128)(2,1)S(1)}, u32[]{:S(2)}, u32[]{:S(2)}) %all-to-all-start.4) | async-done | bytes 32800 | tf_op jit(solution)/shard_map/all_to_all | solution.py:261
  53.4 11.4 %conditional.5 = ((f32[1,16,64]{2,1,0:T(8,128)}, f32[1]{0:T(128)})) conditional(s32[]{:T(128)} %bitcast.3, (bf16[16,8,128]{2,1,0:T(8,128)(2,1)S(1)}, f32[8,128]{1,0:T(8,128)S(1)}, f32[16,64]{1,0:T(8,128)S(1)}, f32[1,16,64]{2,1,0:T(8,128)S(1)}) %tuple.44, (f32[4,1,128]{2,1,0:T(1,128)S(1)}, bf16[16,8,128]{2,1,0:T(8,128)(2,1)S(1)}, ...), branch_computations={%region_5.0_spmd, %region_6.0_spmd} | conditional | bytes 2113544 | solution.py:263
  53.4 0.1 judge.3
  53.5 10.6 %all_to_all.24.parts = f32[16,1,128]{2,1,0:T(1,128)S(1)} all-to-all(f32[16,1,128]{2,1,0:T(1,128)S(1)} %judge.3), channel_id=1, replica_groups=mesh['far'=4,'near'=4,'core'=2,'y'=4,'x'=4] {'y','x'}, dimensions={0} | all-to-all | bytes 16384 | tf_op jit(solution)/shard_map/cond/branch_0_fun/all_to_all | solution.py:257
  64.1 0.7 %finish.2 = (f32[1,16,64]{2,1,0:T(8,128)}, f32[1]{0:T(128)}) custom-call(f32[16,1,128]{2,1,0:T(1,128)S(1)} %all_to_all.24.parts, bf16[16,8,128]{2,1,0:T(8,128)(2,1)S(1)} %get-tuple-element.37.steps, f32[8,128]{1,0:T(8,128)S(1)} %get-tuple-element.38.first, f32[16,64]{1,0:T(8,128)S(1)} %get-tuple-element.39.start_latent), custom_call_target="tpu_custom_call" | custom-call | bytes 1048576 | tf_op jit(solution)/shard_map/cond/branch_0_fun/finish/pallas_call | solution.py:248
  (5 shorter events, 0.0 us)
Async XLA Ops:
  0.6 1.4 %copy-start.6 = (f32[1,16,64]{2,1,0:T(8,128)S(1)}, f32[1,16,64]{2,1,0:T(8,128)}, u32[]{:S(2)}) copy-start(f32[1,16,64]{2,1,0:T(8,128)} %latents.1) | copy-start | bytes 12292
  0.6 1.4 %copy-start.4 = (bf16[256,576]{0,1:T(8,128)(2,1)S(1)}, bf16[256,576]{0,1:T(8,128)(2,1)}, u32[]{:S(2)}) copy-start(bf16[256,576]{0,1:T(8,128)(2,1)} %param.19) | copy-start | bytes 884740
  2.0 15.4 %copy-start = (bf16[3072,384]{1,0:T(8,128)(2,1)S(1)}, bf16[3072,384]{1,0:T(8,128)(2,1)}, u32[]{:S(2)}) copy-start(bf16[3072,384]{1,0:T(8,128)(2,1)} %w_up.1) | copy-start | bytes 7077892
  2.0 15.4 %copy-start.1 = (bf16[384,3072]{1,0:T(8,128)(2,1)S(1)}, bf16[384,3072]{1,0:T(8,128)(2,1)}, u32[]{:S(2)}) copy-start(bf16[384,3072]{1,0:T(8,128)(2,1)} %w_down.1) | copy-start | bytes 7077892
  2.1 15.4 %copy-start.2 = (bf16[64,3072]{1,0:T(8,128)(2,1)S(1)}, bf16[64,3072]{1,0:T(8,128)(2,1)}, u32[]{:S(2)}) copy-start(bf16[64,3072]{1,0:T(8,128)(2,1)} %w_in.1) | copy-start | bytes 1179652
  2.1 15.4 %copy-start.3 = (bf16[3072,64]{0,1:T(8,128)(2,1)S(1)}, bf16[3072,64]{0,1:T(8,128)(2,1)}, u32[]{:S(2)}) copy-start(bf16[3072,64]{0,1:T(8,128)(2,1)} %param.23) | copy-start | bytes 1179652
  17.5 14.3 %copy-start.5 = (f32[16,64]{1,0:T(8,128)S(1)}, f32[16,64]{1,0:T(8,128)}, u32[]{:S(2)}) copy-start(f32[16,64]{1,0:T(8,128)} %param.16) | copy-start | bytes 12292
  31.8 21.6 %all-to-all-start.4 = ((bf16[16,8,128]{2,1,0:T(8,128)(2,1)}), bf16[16,8,128]{2,1,0:T(8,128)(2,1)S(1)}, u32[]{:S(2)}, u32[]{:S(2)}) async-start(bf16[16,8,128]{2,1,0:T(8,128)(2,1)} %get-tuple-element.58), calls=%async_computation.4 | async-start | bytes 65536 | tf_op jit(solution)/shard_map/all_to_all | solution.py:261

commit v10 on v9

--- a/solution.py
+++ b/solution.py
@@ -162,18 +162,18 @@
     return total
 
 
-def judge(steps, first, start_latent, latents, sent):
-    change = fold(start_latent[...] - latents[0]) + before(steps, first)
+def judge(steps, first, start_latent, latents, sent, rows):
+    half = LANES // 2
+    change = before(steps, first)
+    rows[...] = start_latent[...] + jnp.concatenate([change[:, :half], change[:, half:]], axis=0)
+    change = fold(start_latent[...] - latents[0]) + change
     count = change.size * lax.axis_size(TP)
     part = jnp.sum(change * change, axis=0, keepdims=True) / count
     sent[...] = jnp.broadcast_to(part, sent.shape)
 
 
-def finish(parts, steps, first, start_latent, new_latents, step_error):
-    half = LANES // 2
-    change = before(steps, first)
-    change = jnp.concatenate([change[:, :half], change[:, half:]], axis=0)
-    new_latents[0] = start_latent[...] + change
+def finish(parts, rows, new_latents, step_error):
+    new_latents[0] = rows[...]
     step_error[0] = jnp.sum(parts[...])
 
 
@@ -230,37 +230,40 @@
     )(parts)
 
     def errors(steps, *shape):
+        rows = jax.ShapeDtypeStruct((tok_rows, channels), F32)
         return call(
             judge,
-            jax.ShapeDtypeStruct(shape + (LANES,), F32),
+            [jax.ShapeDtypeStruct(shape + (LANES,), F32), rows],
             [VMEM] * 4,
             "judge",
         )(steps, first, start_latent, latents)
 
     def ahead(close):
-        return errors(lax.all_to_all(close, "near", 0, 0, tiled=True), MODS_AT)
+        return tuple(errors(lax.all_to_all(close, "near", 0, 0, tiled=True), MODS_AT))
 
     def gather(part):
         part = jnp.sum(lax.all_gather(part[:1], "x"), axis=0)
         return lax.all_gather(part, "y")
 
-    def close_up(parts, steps):
+    def close_up(parts, rows):
         return call(
             finish,
             (jax.ShapeDtypeStruct(latents.shape, F32), jax.ShapeDtypeStruct((1,), F32)),
-            [VMEM] * 4,
+            [VMEM] * 2,
             "finish",
             out_specs=(VMEM, SMEM),
-        )(parts, steps, first, start_latent)
-
-    def exchange(parts, steps):
-        totals = lax.all_to_all(errors(steps, devices, 1), TP, 0, 0, tiled=True)
-        return close_up(totals, steps)
-
-    part = lax.cond(early, ahead, lambda close: first, close)
+        )(parts, rows)
+
+    def exchange(parts, rows, steps):
+        parts, rows = errors(steps, devices, 1)
+        return close_up(lax.all_to_all(parts, TP, 0, 0, tiled=True), rows)
+
+    part, rows = lax.cond(early, ahead, lambda close: (first, start_latent), close)
     steps = lax.all_to_all(sent, AXES[:2], 0, 0, tiled=True)
     soon = lax.cond(early, gather, lambda part: part[: lax.axis_size("y"), None], part)
-    new_latents, step_error = lax.cond(early, close_up, exchange, soon, steps)
+    new_latents, step_error = lax.cond(
+        early, lambda parts, rows, steps: close_up(parts, rows), exchange, soon, rows, steps
+    )
     return (new_latents, step_error)
 
 

time: 65.1 us -> 65.1 us (level)
  no operation moved by 1% of the time
where the time goes in v10:
time: 65.1 us; the launch traced here: 64.8 us
  blocking collectives  36.5 us (56%)
  starting transfers between devices  13.9 us (21%)
  waiting for transfers between devices  7.76 us (12%)
  Pallas kernels  4.5 us (7%)
  between operations  2.09 us (3%)
    all_to_all x1, blocking collectives, local(): got = lax.all_to_all(sent, TP, 0, 0, tiled=True)  15.1 us
    all_to_all x1, starting transfers between devices, local(): steps = lax.all_to_all(sent, AXES[:2], 0, 0, tiled=True)  13.9 us
    all_to_all x1, blocking collectives, local(): parts = lax.all_to_all(sent, AXES[2:], 0, 0, tiled=True)  10.8 us
    all_to_all x1, blocking collectives, exchange(): return close_up(lax.all_to_all(parts, TP, 0, 0, tiled=True), rows)  10.6 us
    all_to_all x1, waiting for transfers between devices, local(): steps = lax.all_to_all(sent, AXES[:2], 0, 0, tiled=True)  7.76 us
    pallas_call x1, Pallas kernels, local(): call(block, jax.ShapeDtypeStruct((2, devices, MODS_AT, LANES), BF16), [VM...  2.85 us
  transfers between devices with their start and end apart: 1, of which 1 were waited for; matrix products, arithmetic and copies ran while one was open for 0% of the time, Pallas kernels for 0%

profile of v10, /device:TPU:128, one launch (start us, length us, event | category | flops | bytes accessed | tf_op | source)
XLA Modules:
  0.0 64.8 jit_solution(5765037596638503948)
XLA Ops:
  0.6 0.0 copy-start.6
  0.6 0.0 copy-start.4
  2.0 0.0 copy-done.6
  2.0 0.0 copy-done.4
  2.0 0.0 copy-start
  2.0 0.0 copy-start.1
  2.1 0.0 copy-start.2
  2.1 0.0 copy-start.3
  2.1 0.3 prepare.1
  2.4 15.1 %all_to_all.25.got = f32[16,16,128]{2,1,0:T(8,128)S(1)} all-to-all(f32[16,16,128]{2,1,0:T(8,128)S(1)} %get-tuple-element.61), channel_id=1, replica_groups=mesh['far'=4,'near'=4,'core'=2,'y'=4,'x'=4] {'y','x'}, dimensions={0} | all-to-all | bytes 262144 | tf_op jit(solution)/shard_map/all_to_all | solution.py:209
  17.4 0.0 copy-done
  17.4 0.0 copy-done.1
  17.4 0.0 copy-done.2
  17.5 0.0 copy-done.3
  17.5 0.0 copy-start.5
  17.5 2.8 %block.1 = bf16[2,16,8,128]{3,2,1,0:T(8,128)(2,1)S(1)} custom-call(f32[16,16,128]{2,1,0:T(8,128)S(1)} %all_to_all.25.got, f32[8,128]{1,0:T(8,128)S(1)} %get-tuple-element.62.factor, bf16[64,3072]{1,0:T(8,128)(2,1)S(1)} %copy-done.2, bf16[64,3072]{1,0:T(8,128)(2,1)S(1)} %bitcast.9, bf16[3072,384]{1,0:T(8,128)(2,1)S(1)} %copy-done, bf16[384,3072]{1,0:T(8,128)(2,1)S(1)} %copy-done.1), custom_call_target="tpu_custom_call" | custom-call | flops 855638016 | bytes 1048576 | tf_op jit(solution)/shard_map/block/pallas_call | solution.py:210
  20.3 10.8 %all_to_all.26 = bf16[32,8,128]{2,1,0:T(8,128)(2,1)S(1)} all-to-all(bf16[32,8,128]{2,1,0:T(8,128)(2,1)S(1)} %bitcast.10), channel_id=1, replica_groups=mesh['far'=4,'near'=4,'core'=2,'y'=4,'x'=4] {'core','y','x'}, dimensions={0} | all-to-all | bytes 131072 | tf_op jit(solution)/shard_map/all_to_all | solution.py:223
  31.2 0.6 combine.1
  31.8 0.0 copy-done.5
  31.8 13.9 %all-to-all-start.4 = ((bf16[16,8,128]{2,1,0:T(8,128)(2,1)}), bf16[16,8,128]{2,1,0:T(8,128)(2,1)S(1)}, u32[]{:S(2)}, u32[]{:S(2)}) async-start(bf16[16,8,128]{2,1,0:T(8,128)(2,1)} %get-tuple-element.63), calls=%async_computation.4 | async-start | bytes 65536 | tf_op jit(solution)/shard_map/all_to_all | solution.py:262
  45.7 7.8 %all-to-all-done.4 = bf16[16,8,128]{2,1,0:T(8,128)(2,1)S(1)} async-done(((bf16[16,8,128]{2,1,0:T(8,128)(2,1)}), bf16[16,8,128]{2,1,0:T(8,128)(2,1)S(1)}, u32[]{:S(2)}, u32[]{:S(2)}) %all-to-all-start.4) | async-done | bytes 32800 | tf_op jit(solution)/shard_map/all_to_all | solution.py:262
  53.4 11.4 %conditional.5 = ((f32[1,16,64]{2,1,0:T(8,128)}, f32[1]{0:T(128)})) conditional(s32[]{:T(128)} %bitcast.3, (bf16[16,8,128]{2,1,0:T(8,128)(2,1)S(1)}, f32[8,128]{1,0:T(8,128)S(1)}, f32[16,64]{1,0:T(8,128)S(1)}, f32[1,16,64]{2,1,0:T(8,128)S(1)}) %tuple.50, (f32[4,1,128]{2,1,0:T(1,128)S(1)}, f32[16,64]{1,0:T(8,128)S(1)}) %tuple.33), branch_computations={%region_5.0_spmd, %region_6.0_spmd} | conditional | bytes 2113544 | solution.py:264
  53.4 0.1 judge.3
  53.5 10.6 %all_to_all.24.parts = f32[16,1,128]{2,1,0:T(1,128)S(1)} all-to-all(f32[16,1,128]{2,1,0:T(1,128)S(1)} %get-tuple-element.44), channel_id=1, replica_groups=mesh['far'=4,'near'=4,'core'=2,'y'=4,'x'=4] {'y','x'}, dimensions={0} | all-to-all | bytes 16384 | tf_op jit(solution)/shard_map/cond/branch_0_fun/all_to_all | solution.py:259
  64.1 0.6 %finish.2 = (f32[1,16,64]{2,1,0:T(8,128)}, f32[1]{0:T(128)}) custom-call(f32[16,1,128]{2,1,0:T(1,128)S(1)} %all_to_all.24.parts, f32[16,64]{1,0:T(8,128)S(1)} %get-tuple-element.45.rows), custom_call_target="tpu_custom_call" | custom-call | bytes 1048576 | tf_op jit(solution)/shard_map/cond/branch_0_fun/finish/pallas_call | solution.py:249
  (6 shorter events, 0.0 us)
Async XLA Ops:
  0.6 1.4 %copy-start.6 = (f32[1,16,64]{2,1,0:T(8,128)S(1)}, f32[1,16,64]{2,1,0:T(8,128)}, u32[]{:S(2)}) copy-start(f32[1,16,64]{2,1,0:T(8,128)} %latents.1) | copy-start | bytes 12292
  0.6 1.4 %copy-start.4 = (bf16[256,576]{0,1:T(8,128)(2,1)S(1)}, bf16[256,576]{0,1:T(8,128)(2,1)}, u32[]{:S(2)}) copy-start(bf16[256,576]{0,1:T(8,128)(2,1)} %param.19) | copy-start | bytes 884740
  2.0 15.4 %copy-start = (bf16[3072,384]{1,0:T(8,128)(2,1)S(1)}, bf16[3072,384]{1,0:T(8,128)(2,1)}, u32[]{:S(2)}) copy-start(bf16[3072,384]{1,0:T(8,128)(2,1)} %w_up.1) | copy-start | bytes 7077892
  2.0 15.4 %copy-start.1 = (bf16[384,3072]{1,0:T(8,128)(2,1)S(1)}, bf16[384,3072]{1,0:T(8,128)(2,1)}, u32[]{:S(2)}) copy-start(bf16[384,3072]{1,0:T(8,128)(2,1)} %w_down.1) | copy-start | bytes 7077892
  2.1 15.4 %copy-start.2 = (bf16[64,3072]{1,0:T(8,128)(2,1)S(1)}, bf16[64,3072]{1,0:T(8,128)(2,1)}, u32[]{:S(2)}) copy-start(bf16[64,3072]{1,0:T(8,128)(2,1)} %w_in.1) | copy-start | bytes 1179652
  2.1 15.4 %copy-start.3 = (bf16[3072,64]{0,1:T(8,128)(2,1)S(1)}, bf16[3072,64]{0,1:T(8,128)(2,1)}, u32[]{:S(2)}) copy-start(bf16[3072,64]{0,1:T(8,128)(2,1)} %param.23) | copy-start | bytes 1179652
  17.5 14.3 %copy-start.5 = (f32[16,64]{1,0:T(8,128)S(1)}, f32[16,64]{1,0:T(8,128)}, u32[]{:S(2)}) copy-start(f32[16,64]{1,0:T(8,128)} %param.16) | copy-start | bytes 12292
  31.8 21.6 %all-to-all-start.4 = ((bf16[16,8,128]{2,1,0:T(8,128)(2,1)}), bf16[16,8,128]{2,1,0:T(8,128)(2,1)S(1)}, u32[]{:S(2)}, u32[]{:S(2)}) async-start(bf16[16,8,128]{2,1,0:T(8,128)(2,1)} %get-tuple-element.63), calls=%async_computation.4 | async-start | bytes 65536 | tf_op jit(solution)/shard_map/all_to_all | solution.py:262

commit v11 on v8

--- a/solution.py
+++ b/solution.py
@@ -85,14 +85,6 @@
         pairs += even[:4] + [even[4] + odd[0]] + odd[1:]
     shift, scale, gate = pairs[:count], pairs[count : 2 * count], pairs[2 * count :]
     dims = (((1,), (1,)), ((), ()))
-    gated = w_out_t[...].astype(F32) * jnp.concatenate(gate, axis=1)
-    high, low = split(gated)
-    gated = jnp.concatenate([high, low], axis=0).astype(BF16)
-    down = lax.dot_general(w_down[...], gated, dims, preferred_element_type=F32)
-    down = down + swap(down)
-    high, low = split(down)
-    down = jnp.where(left(down.shape), high, low).astype(BF16)
-
     lat = got[:, :MODS_AT, :].reshape(devices * MODS_AT, LANES)
     lat = jnp.concatenate([lat[:, : LANES // 2], lat[:, LANES // 2 :]], axis=0).astype(BF16)
     tokens = lat.shape[0]
@@ -120,6 +112,13 @@
     own = jnp.concatenate([high, rest, last], axis=0).astype(BF16)
     own = lax.dot_general(own, w_out_t[...], dims, preferred_element_type=F32)
     own = fold(own[:16] + own[16:32] + own[32:48])
+    gated = w_out_t[...].astype(F32) * jnp.concatenate(gate, axis=1)
+    high, low = split(gated)
+    gated = jnp.concatenate([high, low], axis=0).astype(BF16)
+    down = lax.dot_general(w_down[...], gated, dims, preferred_element_type=F32)
+    down = down + swap(down)
+    high, low = split(down)
+    down = jnp.where(left(down.shape), high, low).astype(BF16)
     spread = jnp.sum(total, axis=1, keepdims=True) / width
     inverse = 1.0 / jnp.sqrt(spread + 1e-06)
     for i in range(count):

time: 65.1 us -> 65.2 us (level)
  no operation moved by 1% of the time
where the time goes in v11:
time: 65.2 us; the launch traced here: 64.9 us
  blocking collectives  36.5 us (56%)
  starting transfers between devices  13.9 us (21%)
  waiting for transfers between devices  7.76 us (12%)
  Pallas kernels  4.61 us (7%)
  between operations  2.09 us (3%)
    all_to_all x1, blocking collectives, local(): got = lax.all_to_all(sent, TP, 0, 0, tiled=True)  15.1 us
    all_to_all x1, starting transfers between devices, local(): steps = lax.all_to_all(sent, AXES[:2], 0, 0, tiled=True)  13.9 us
    all_to_all x1, blocking collectives, local(): parts = lax.all_to_all(sent, AXES[2:], 0, 0, tiled=True)  10.8 us
    all_to_all x1, blocking collectives, exchange(): totals = lax.all_to_all(errors(steps, devices, 1), TP, 0, 0, tiled=True)  10.6 us
    all_to_all x1, waiting for transfers between devices, local(): steps = lax.all_to_all(sent, AXES[:2], 0, 0, tiled=True)  7.76 us
    pallas_call x1, Pallas kernels, local(): call(block, jax.ShapeDtypeStruct((2, devices, MODS_AT, LANES), BF16), [VM...  2.9 us
  transfers between devices with their start and end apart: 1, of which 1 were waited for; matrix products, arithmetic and copies ran while one was open for 0% of the time, Pallas kernels for 0%

profile of v11, /device:TPU:128, one launch (start us, length us, event | category | flops | bytes accessed | tf_op | source)
XLA Modules:
  0.0 64.9 jit_solution(14573417151174404151)
XLA Ops:
  0.6 0.0 copy-start.4
  0.6 0.0 copy-start.6
  2.0 0.0 copy-done.4
  2.0 0.0 copy-done.6
  2.0 0.0 copy-start
  2.0 0.0 copy-start.1
  2.0 0.0 copy-start.2
  2.1 0.0 copy-start.3
  2.1 0.3 prepare.1
  2.3 15.1 %all_to_all.25.got = f32[16,16,128]{2,1,0:T(8,128)S(1)} all-to-all(f32[16,16,128]{2,1,0:T(8,128)S(1)} %get-tuple-element.52), channel_id=1, replica_groups=mesh['far'=4,'near'=4,'core'=2,'y'=4,'x'=4] {'y','x'}, dimensions={0} | all-to-all | bytes 262144 | tf_op jit(solution)/shard_map/all_to_all | solution.py:203
  17.4 0.0 copy-done
  17.4 0.0 copy-done.1
  17.4 0.0 copy-done.2
  17.4 0.0 copy-done.3
  17.5 0.0 copy-start.5
  17.5 2.9 %block.1 = bf16[2,16,8,128]{3,2,1,0:T(8,128)(2,1)S(1)} custom-call(f32[16,16,128]{2,1,0:T(8,128)S(1)} %all_to_all.25.got, f32[8,128]{1,0:T(8,128)S(1)} %get-tuple-element.53.factor, bf16[64,3072]{1,0:T(8,128)(2,1)S(1)} %copy-done.2, bf16[64,3072]{1,0:T(8,128)(2,1)S(1)} %bitcast.9, bf16[3072,384]{1,0:T(8,128)(2,1)S(1)} %copy-done, bf16[384,3072]{1,0:T(8,128)(2,1)S(1)} %copy-done.1), custom_call_target="tpu_custom_call" | custom-call | flops 855638016 | bytes 1048576 | tf_op jit(solution)/shard_map/block/pallas_call | solution.py:204
  20.4 10.8 %all_to_all.26 = bf16[32,8,128]{2,1,0:T(8,128)(2,1)S(1)} all-to-all(bf16[32,8,128]{2,1,0:T(8,128)(2,1)S(1)} %bitcast.10), channel_id=1, replica_groups=mesh['far'=4,'near'=4,'core'=2,'y'=4,'x'=4] {'core','y','x'}, dimensions={0} | all-to-all | bytes 131072 | tf_op jit(solution)/shard_map/all_to_all | solution.py:217
  31.2 0.6 combine.1
  31.8 0.0 copy-done.5
  31.8 13.9 %all-to-all-start.4 = ((bf16[16,8,128]{2,1,0:T(8,128)(2,1)}), bf16[16,8,128]{2,1,0:T(8,128)(2,1)S(1)}, u32[]{:S(2)}, u32[]{:S(2)}) async-start(bf16[16,8,128]{2,1,0:T(8,128)(2,1)} %get-tuple-element.54), calls=%async_computation.4 | async-start | bytes 65536 | tf_op jit(solution)/shard_map/all_to_all | solution.py:255
  45.7 7.8 %all-to-all-done.4 = bf16[16,8,128]{2,1,0:T(8,128)(2,1)S(1)} async-done(((bf16[16,8,128]{2,1,0:T(8,128)(2,1)}), bf16[16,8,128]{2,1,0:T(8,128)(2,1)S(1)}, u32[]{:S(2)}, u32[]{:S(2)}) %all-to-all-start.4) | async-done | bytes 32800 | tf_op jit(solution)/shard_map/all_to_all | solution.py:255
  53.5 11.4 %conditional.5 = ((f32[1,16,64]{2,1,0:T(8,128)}, f32[1]{0:T(128)})) conditional(s32[]{:T(128)} %convert_element_type.2, (bf16[16,8,128]{2,1,0:T(8,128)(2,1)S(1)}, f32[8,128]{1,0:T(8,128)S(1)}, f32[16,64]{1,0:T(8,128)S(1)}, f32[1,16,64]{2,1,0:T(8,128)S(1)}) %tuple.44, (f32[4,1,128]{2,1,0:T(1,128)S(1)}, bf16[16,8,128]{2,1,0:T(8,128)(2,1)S(1)}, ...), branch_computations={%region_5.0_spmd, %region_6.0_spmd} | conditional | bytes 2113544 | solution.py:257
  53.5 0.1 judge.3
  53.6 10.6 %all_to_all.24.parts = f32[16,1,128]{2,1,0:T(1,128)S(1)} all-to-all(f32[16,1,128]{2,1,0:T(1,128)S(1)} %judge.3), channel_id=1, replica_groups=mesh['far'=4,'near'=4,'core'=2,'y'=4,'x'=4] {'y','x'}, dimensions={0} | all-to-all | bytes 16384 | tf_op jit(solution)/shard_map/cond/branch_0_fun/all_to_all | solution.py:251
  64.2 0.7 %finish.2 = (f32[1,16,64]{2,1,0:T(8,128)}, f32[1]{0:T(128)}) custom-call(f32[16,1,128]{2,1,0:T(1,128)S(1)} %all_to_all.24.parts, bf16[16,8,128]{2,1,0:T(8,128)(2,1)S(1)} %get-tuple-element.37.steps, f32[8,128]{1,0:T(8,128)S(1)} %get-tuple-element.38.first, f32[16,64]{1,0:T(8,128)S(1)} %get-tuple-element.39.start_latent), custom_call_target="tpu_custom_call" | custom-call | bytes 1048576 | tf_op jit(solution)/shard_map/cond/branch_0_fun/finish/pallas_call | solution.py:242
  (5 shorter events, 0.0 us)
Async XLA Ops:
  0.6 1.4 %copy-start.4 = (bf16[256,576]{0,1:T(8,128)(2,1)S(1)}, bf16[256,576]{0,1:T(8,128)(2,1)}, u32[]{:S(2)}) copy-start(bf16[256,576]{0,1:T(8,128)(2,1)} %param.19) | copy-start | bytes 884740
  0.6 1.4 %copy-start.6 = (f32[1,16,64]{2,1,0:T(8,128)S(1)}, f32[1,16,64]{2,1,0:T(8,128)}, u32[]{:S(2)}) copy-start(f32[1,16,64]{2,1,0:T(8,128)} %latents.1) | copy-start | bytes 12292
  2.0 15.4 %copy-start = (bf16[3072,384]{1,0:T(8,128)(2,1)S(1)}, bf16[3072,384]{1,0:T(8,128)(2,1)}, u32[]{:S(2)}) copy-start(bf16[3072,384]{1,0:T(8,128)(2,1)} %w_up.1) | copy-start | bytes 7077892
  2.0 15.4 %copy-start.1 = (bf16[384,3072]{1,0:T(8,128)(2,1)S(1)}, bf16[384,3072]{1,0:T(8,128)(2,1)}, u32[]{:S(2)}) copy-start(bf16[384,3072]{1,0:T(8,128)(2,1)} %w_down.1) | copy-start | bytes 7077892
  2.0 15.4 %copy-start.2 = (bf16[64,3072]{1,0:T(8,128)(2,1)S(1)}, bf16[64,3072]{1,0:T(8,128)(2,1)}, u32[]{:S(2)}) copy-start(bf16[64,3072]{1,0:T(8,128)(2,1)} %w_in.1) | copy-start | bytes 1179652
  2.1 15.4 %copy-start.3 = (bf16[3072,64]{0,1:T(8,128)(2,1)S(1)}, bf16[3072,64]{0,1:T(8,128)(2,1)}, u32[]{:S(2)}) copy-start(bf16[3072,64]{0,1:T(8,128)(2,1)} %param.23) | copy-start | bytes 1179652
  17.5 14.4 %copy-start.5 = (f32[16,64]{1,0:T(8,128)S(1)}, f32[16,64]{1,0:T(8,128)}, u32[]{:S(2)}) copy-start(f32[16,64]{1,0:T(8,128)} %param.16) | copy-start | bytes 12292
  31.8 21.6 %all-to-all-start.4 = ((bf16[16,8,128]{2,1,0:T(8,128)(2,1)}), bf16[16,8,128]{2,1,0:T(8,128)(2,1)S(1)}, u32[]{:S(2)}, u32[]{:S(2)}) async-start(bf16[16,8,128]{2,1,0:T(8,128)(2,1)} %get-tuple-element.54), calls=%async_computation.4 | async-start | bytes 65536 | tf_op jit(solution)/shard_map/all_to_all | solution.py:255
